TPU v7x, 512 devices: a whole 4x4x16 slice. The times are simulated.
512 devices in a mesh: ctx: 64 (over y, z), head: 8 (over x, core).
Axes of the slice: x: 4, y: 4, z: 16, core: 2. Of those that a mesh axis runs over, the one named last changes fastest.
Arguments:
- queries: bfloat16 [16384, 4096], P('ctx', 'head'), may hold values from -144 to 144
- keys: bfloat16 [16384, 1024], P('ctx', 'head'), may hold values from -6 to 6
- values: bfloat16 [16384, 1024], P('ctx', 'head'), may hold values from -6 to 6
- block_ids: int32 [16384], P('ctx'), may hold values from 0 to 1023, as said below
- out_weight: bfloat16 [4096, 4096], P('head'), may hold values from -0.09375 to 0.09375
Outputs:
- mixed: bfloat16 [16384, 4096], P('ctx', 'head')
Inputs may be any that keep to these rules, and one draw needn't show every extreme that they name: `block_ids`: block numbers never fall along the sequence; each number of 0 to 1023 names 1 to 32 tokens, and one names exactly 32.
All inputs are finite; a program needn't handle non-finite values.
Results may differ from a plain program's by a relative error of at most 0.02.
Values may be sent and summed in bfloat16 or wider, within the bound.
No kernel may reach another device: no remote copies, remote signals or barrier semaphores. Data moves between devices by JAX's collectives and lax.ppermute only.
A program may use at most 64 MiB of HBM per device.

v0:
```python
import jax
import jax.numpy as jnp
from jax import lax
from jax.sharding import PartitionSpec as P

HEAD_SIZE = 128


def attend_block(state, heads_of_queries, query_ids, key_block, value_block, key_ids):
    running_max, running_total, running_sum = state
    scale = HEAD_SIZE ** (-0.5)
    scores = (
        jnp.einsum(
            "tkgd,pkd->kgtp", heads_of_queries, key_block, preferred_element_type=jnp.float32
        )
        * scale
    )
    visible = key_ids[None, :] <= query_ids[:, None]
    scores = jnp.where(visible, scores, -1e30)
    new_max = jnp.maximum(running_max, jnp.max(scores, axis=-1))
    expo = jnp.where(visible, jnp.exp(scores - new_max[..., None]), 0.0)
    factor = jnp.exp(running_max - new_max)
    new_total = running_total * factor + jnp.sum(expo, axis=-1)
    new_sum = running_sum * factor[..., None] + jnp.einsum(
        "kgtp,pkd->kgtd", expo.astype(jnp.bfloat16), value_block, preferred_element_type=jnp.float32
    )
    return (new_max, new_total, new_sum)


def local(queries, keys, values, block_ids, out_weight):
    rows = queries.shape[0]
    half_rows = rows // 2
    heads_here = queries.shape[1] // HEAD_SIZE
    kv_here = keys.shape[1] // HEAD_SIZE
    query_group = heads_here // kv_here
    early_queries = queries[:half_rows]
    later_queries = queries[half_rows:]
    early_ids = block_ids[:half_rows]
    later_ids = block_ids[half_rows:]
    span_data = [
        (early_queries.reshape(half_rows, kv_here, query_group, HEAD_SIZE), early_ids),
        (later_queries.reshape(half_rows, kv_here, query_group, HEAD_SIZE), later_ids),
    ]

    def fresh_state():
        return (
            jnp.full((kv_here, query_group, half_rows), -1e30, jnp.float32),
            jnp.zeros((kv_here, query_group, half_rows), jnp.float32),
            jnp.zeros((kv_here, query_group, half_rows, HEAD_SIZE), jnp.float32),
        )

    carry = (fresh_state(), fresh_state())
    key_piece = lax.all_gather(keys, "ctx", axis=0, tiled=True)
    value_piece = lax.all_gather(values, "ctx", axis=0, tiled=True)
    id_piece = lax.all_gather(block_ids, "ctx", axis=0, tiled=True)
    block_count = key_piece.shape[0] // rows
    key_blocks = key_piece.reshape(block_count, rows, kv_here, HEAD_SIZE)
    value_blocks = value_piece.reshape(block_count, rows, kv_here, HEAD_SIZE)
    id_blocks = id_piece.reshape(block_count, rows)

    def one_block(states, block):
        key_block, value_block, key_ids = block
        updated = []
        for span_number in range(2):
            heads_of_queries, query_ids = span_data[span_number]

            def apply_block(state, heads_of_queries=heads_of_queries, query_ids=query_ids):
                return attend_block(
                    state, heads_of_queries, query_ids, key_block, value_block, key_ids
                )

            updated.append(
                lax.cond(
                    jnp.min(key_ids) > jnp.max(query_ids),
                    lambda state: state,
                    apply_block,
                    states[span_number],
                )
            )
        return ((updated[0], updated[1]), None)

    carry, unused = lax.scan(one_block, carry, (key_blocks, value_blocks, id_blocks))

    def finish(state):
        running_max, running_total, running_sum = state
        attended = running_sum / running_total[..., None]
        attended = jnp.transpose(attended, (2, 0, 1, 3)).reshape(half_rows, heads_here * HEAD_SIZE)
        return attended.astype(jnp.bfloat16)

    early_out = finish(carry[0])
    later_out = finish(carry[1])
    attended_rows = jnp.concatenate([early_out, later_out], axis=0)
    partial_value = jnp.dot(attended_rows, out_weight, preferred_element_type=jnp.float32)
    return lax.psum_scatter(
        partial_value.astype(jnp.bfloat16), "head", scatter_dimension=1, tiled=True
    )


def solution(mesh):
    return jax.shard_map(
        local,
        mesh=mesh,
        in_specs=(P("ctx", "head"), P("ctx", "head"), P("ctx", "head"), P("ctx"), P("head", None)),
        out_specs=P("ctx", "head"),
        check_vma=False,
    )
```

profile of v0, /device:TPU:1, one launch (start us, length us, event | category | flops | bytes accessed | tf_op | source)
XLA Modules:
  0.0 718.1 jit_solution(7698934992700356358)
XLA Ops:
  8.1 1.0 fusion.37
  9.6 73.9 %all-gather = s32[64,1,256]{2,1,0:T(1,128)S(1)} all-gather(s32[1,1,256]{2,1,0:T(1,128)} %bitcast.113), channel_id=1, replica_groups=mesh['ctx'=64,'head'=8] {'ctx'}, dimensions={0}, use_global_device_ids=true | all-gather | bytes 66560 | tf_op jit(solution)/shard_map/all_gather | solution.py:55
  83.5 1.4 slice_reduce_fusion
  84.9 69.3 %all-gather.4.cloned.1.call-done = bf16[16384,128]{1,0:T(8,128)(2,1)} async-done(((bf16[256,128]{1,0:T(8,128)(2,1)}), bf16[16384,128]{1,0:T(8,128)(2,1)}) %all-gather.4.cloned.1.call-update) | async-done | bytes 4194320 | tf_op jit(solution)/shard_map/all_gather | solution.py:53
  154.2 144.2 %all-gather.6.cloned.1.call-done = bf16[16384,128]{1,0:T(8,128)(2,1)} async-done(((bf16[256,128]{1,0:T(8,128)(2,1)}), bf16[16384,128]{1,0:T(8,128)(2,1)}) %all-gather.6.cloned.1.call-update) | async-done | bytes 4194320 | tf_op jit(solution)/shard_map/all_gather | solution.py:54
  298.5 265.1 %while.21 = (s32[]{:T(128)}, f32[1,4,128]{2,1,0:T(4,128)S(1)}, f32[1,4,128]{2,1,0:T(4,128)S(1)}, f32[1,4,128,128]{3,2,1,0:T(8,128)S(1)}, f32[1,4,128]{2,1,0:T(4,...) while((s32[]{:T(128)}, f32[1,4,128]{2,1,0:T(4,128)S(1)}, ...), condition=%wide.region_12.13_spmd, body=%wide.region_2.12_spmd.sunk | while | flops 136908032 | bytes 5313957 | solution.py:82
  298.5 0.9 dynamic-slice_bitcast_fusion.3
  309.2 0.9 dynamic-slice_bitcast_fusion.3
  313.3 0.9 dynamic-slice_bitcast_fusion.3
  317.4 0.9 dynamic-slice_bitcast_fusion.3
  329.7 0.9 dynamic-slice_bitcast_fusion.3
  333.8 0.9 dynamic-slice_bitcast_fusion.3
  337.9 0.9 dynamic-slice_bitcast_fusion.3
  342.1 0.9 dynamic-slice_bitcast_fusion.3
  346.2 0.9 dynamic-slice_bitcast_fusion.3
  350.3 0.9 dynamic-slice_bitcast_fusion.3
  354.4 0.9 dynamic-slice_bitcast_fusion.3
  358.5 0.9 dynamic-slice_bitcast_fusion.3
  370.8 0.9 dynamic-slice_bitcast_fusion.3
  374.9 0.9 dynamic-slice_bitcast_fusion.3
  379.0 0.9 dynamic-slice_bitcast_fusion.3
  383.1 0.9 dynamic-slice_bitcast_fusion.3
  564.0 4.8 convolution_convert_fusion
  568.8 142.7 %reduce-scatter.2.cloned.1.call-done = bf16[256,512]{1,0:T(8,128)(2,1)} async-done(((bf16[256,4096]{1,0:T(8,128)(2,1)}), bf16[256,512]{1,0:T(8,128)(2,1)}) %reduce-scatter.2.cloned.1.call-update) | async-done | bytes 262160 | tf_op jit(solution)/shard_map/reduce_scatter | solution.py:94
  (532 shorter events, 96.2 us)
Async XLA Ops:
  6.5 147.7 %all-gather.4.cloned.1.call-start = ((), (), s32[]{:S(2)}) async-start(), calls=%async_computation.1 | async-start | bytes 4259840 | tf_op jit(solution)/shard_map/all_gather | solution.py:53
  7.3 291.1 %all-gather.6.cloned.1.call-start = ((), (), s32[]{:S(2)}) async-start(), calls=%async_computation.2 | async-start | bytes 4259840 | tf_op jit(solution)/shard_map/all_gather | solution.py:54
  8.0 703.5 %reduce-scatter.2.cloned.1.call-start = ((), (), s32[]{:S(2)}) async-start(), calls=%async_computation.3 | async-start | bytes 2359296 | tf_op jit(solution)/shard_map/reduce_scatter | solution.py:94
Sparse Core Ops, SparseCore 0:
  10.3 143.8 all-gather.3
  157.2 141.1 all-gather.5
  568.9 142.5 reduce-scatter.1
where the time goes:
time: 724 us; the launch traced here: 718 us
  waiting for transfers between devices  358 us (49%)
  loops' own time  163 us (23%)
  blocking collectives  73.9 us (10%)
  local copies, waits for them, and re-layouts  59.2 us (8%)
  other arithmetic  43.9 us (6%)
  between operations  13.2 us (2%)
    another operation x1, loops' own time, local(): lax.scan(one_block, carry, (key_blocks, value_blocks, id_blocks))  160 us
    all_gather x1, waiting for transfers between devices, local(): value_piece = lax.all_gather(values, 'ctx', axis=0, tiled=True)  144 us
    reduce_scatter x1, waiting for transfers between devices, local(): lax.psum_scatter(partial_value.astype(jnp.bfloat16), 'head', scatter_dime...  143 us
    all_gather x1, blocking collectives, local(): id_piece = lax.all_gather(block_ids, 'ctx', axis=0, tiled=True)  73.9 us
    all_gather x1, waiting for transfers between devices, local(): key_piece = lax.all_gather(keys, 'ctx', axis=0, tiled=True)  69.3 us
    squeeze x64, local copies, waits for them, and re-layouts, local(): lax.scan(one_block, carry, (key_blocks, value_blocks, id_blocks))  56.7 us
    reduce_min x64, other arithmetic, one_block(): jnp.min(key_ids) > jnp.max(query_ids)  41.8 us
  transfers between devices with their start and end apart: 3, of which 3 were waited for; matrix products, arithmetic and copies ran while one was open for 0% of the time, Pallas kernels for 0%

commit v1 on v0

v1 whole, which is shorter than its diff:
```python
import functools

import jax
import jax.numpy as jnp
import numpy as np
from jax import lax
from jax.experimental import pallas as pl
from jax.experimental.pallas import tpu as pltpu
from jax.sharding import Mesh
from jax.sharding import PartitionSpec as P

HEAD = 128
GROUP = 4
TOK = 256
LOG_SCALE = float(128**-0.5 * np.log2(np.e))
HIDDEN = -1e30
FLOOR = -1e29
ROWS = TOK * 2 + 16
QROWS = TOK + 16
OROWS = GROUP * HEAD + 16
VROWS = HEAD + 16
TILE = 4 * TOK
WIDTH = GROUP * HEAD
F32, BF16 = jnp.float32, jnp.bfloat16
NX, NY, NZ = 4, 4, 16


def ring_place(d, z):
    return ((z // 4 - d) % NY) * NZ + z


def ring_step(step):
    return [
        (ring_place(d, (z + step) % NZ), ring_place(d, z)) for d in range(4) for z in range(NZ)
    ]


def ring_groups():
    return [
        [i * NZ + ((i + d) % 4) * 4 + zl for i in range(4)] for d in range(4) for zl in range(4)
    ]


def schedule():
    table = np.zeros((NY * NZ, 32), np.int32)
    for y in range(NY):
        for z in range(NZ):
            zh, zl = divmod(z, 4)
            d = (zh - y) % 4
            full = [(q, i) for q in range(4) for i in range(q)]
            row = table[y * NZ + z]
            for q in range(4):
                quad = (q + d) % 4
                if quad < zh:
                    full.append((q, q))
                elif quad == zh:
                    row[1] = q
                after = q * NZ + z + 1
                if zl == 3 and after < NY * NZ:
                    i, rest = divmod(after, NZ)
                    if (i + d) % 4 == rest // 4:
                        row[2:5] = 1, q, i
            row[0] = len(full)
            for n, (q, i) in enumerate(full):
                row[8 + n] = q
                row[20 + n] = i
    return table


def dot(a, b, dims):
    return lax.dot_general(a, b, (dims, ((), ())), preferred_element_type=F32)


def attend_kernel(
    info, q_ref, own, ahead, behind, far_low, far_high, out_ref,
    k_buf, v_buf, s0, s1, top, acc, row_max, ids,
):
    sides = (own, ahead, behind)
    for i in range(4):
        for n in range(4):
            if n < 3:
                block = sides[n].at[i]
            else:
                block = (far_low if i < 2 else far_high).at[i % 2]
            k_buf[i, n * TOK : (n + 1) * TOK, :] = block[0:TOK, :]
            v_buf[i, 0:HEAD, n * TOK : (n + 1) * TOK] = block[TOK : 2 * TOK, :].T
        v_buf[i, HEAD:VROWS, :] = jnp.ones((16, TILE), BF16)
    acc[...] = jnp.zeros_like(acc)
    row_max[...] = jnp.full_like(row_max, FLOOR)
    scores = (s0, s1)
    parts = TILE // TOK

    def query(q, h):
        return q_ref[q, 0:TOK, h * HEAD : (h + 1) * HEAD]

    def score_part(q, i, h, c):
        return dot(k_buf[i, c * TOK : (c + 1) * TOK, :], query(q, h), ((1,), (1,)))

    def fold(s):
        return jnp.max(s.reshape(TOK // 8, 8, TOK), axis=0)

    best = None
    for c in range(parts):
        s = score_part(info[8], info[20], 0, c)
        s0[c * TOK : (c + 1) * TOK, :] = s
        best = fold(s) if best is None else jnp.maximum(best, fold(s))
    top[...] = best

    def tile(n, carry):
        q, i = info[8 + n], info[20 + n]
        after = jnp.minimum(n + 1, info[0] - 1)
        q_after, i_after = info[8 + after], info[20 + after]
        for h in range(GROUP):
            now, later = scores[h % 2], scores[(h + 1) % 2]
            q_n, i_n, h_n = (q, i, h + 1) if h < GROUP - 1 else (q_after, i_after, 0)
            old = row_max[q, h : h + 1, :]
            new = jnp.maximum(old, jnp.max(top[...], axis=0, keepdims=True))
            factor = jnp.exp2((old - new) * LOG_SCALE)
            row_max[q, h : h + 1, :] = new
            best = None
            total = acc[q, h] * factor
            for c in range(parts):
                rows = slice(c * TOK, (c + 1) * TOK)
                s = score_part(q_n, i_n, h_n, c)
                later[rows, :] = s
                best = fold(s) if best is None else jnp.maximum(best, fold(s))
                weights = jnp.exp2((now[rows, :] - new) * LOG_SCALE).astype(BF16)
                total = total + dot(v_buf[i, :, rows], weights, ((1,), (0,)))
            acc[q, h] = total
            top[...] = best
        return carry

    lax.fori_loop(0, info[0], tile, 0)

    def masked(q, i, first, size):
        q_ids = (
            q_ref[q, TOK : TOK + 16, 0:TOK].astype(F32) * 32.0
            + q_ref[q, TOK : TOK + 16, TOK : 2 * TOK].astype(F32)
        )[0:1, :]
        hidden = jnp.where(
            jnp.concatenate([ids[0:size, :]] * 2, axis=1) <= q_ids, 0.0, HIDDEN
        )
        for h in range(GROUP):
            s = dot(k_buf[i, first : first + size, :], query(q, h), ((1,), (1,)))
            s = jnp.where(hidden < 0.0, HIDDEN, s)
            old = row_max[q, h : h + 1, :]
            new = jnp.maximum(old, jnp.max(s, axis=0, keepdims=True))
            factor = jnp.exp2((old - new) * LOG_SCALE)
            row_max[q, h : h + 1, :] = new
            weights = jnp.exp2((s - new) * LOG_SCALE).astype(BF16)
            acc[q, h] = acc[q, h] * factor + dot(
                v_buf[i, :, first : first + size], weights, ((1,), (0,))
            )

    def spread_ids(block, at):
        rows = block[2 * TOK : 2 * TOK + 16, :].astype(F32)
        for half in range(2):
            line = rows[half : half + 1, :] * 32.0 + rows[half + 2 : half + 3, :]
            ids[at + half * 128 : at + half * 128 + 128, :] = jnp.broadcast_to(line, (128, 128)).T

    mq = info[1]
    for n in range(3):
        spread_ids(sides[n].at[mq], n * TOK)

    @pl.when(mq < 2)
    def _():
        spread_ids(far_low.at[jnp.minimum(mq, 1)], 3 * TOK)

    @pl.when(mq >= 2)
    def _():
        spread_ids(far_high.at[jnp.maximum(mq - 2, 0)], 3 * TOK)

    masked(mq, mq, 0, TILE)

    @pl.when(info[2] == 1)
    def _():
        spread_ids(ahead.at[info[4]], 0)
        masked(info[3], info[4], TOK, TOK)

    for q in range(4):
        sums = []
        for h in range(GROUP):
            total = jnp.maximum(acc[q, h, HEAD : HEAD + 1, :], 0.5)
            out_ref[q, h * HEAD : (h + 1) * HEAD, :] = (
                acc[q, h, 0:HEAD, :] * (1.0 / total)
            ).astype(BF16)
            sums.append(row_max[q, h : h + 1, :] * LOG_SCALE + jnp.log2(total))
        log_sum = jnp.concatenate(sums, axis=0)
        high = log_sum.astype(BF16).astype(F32)
        mid = (log_sum - high).astype(BF16).astype(F32)
        low = log_sum - high - mid
        out_ref[q, GROUP * HEAD : OROWS, :] = jnp.concatenate(
            [high, mid, low, jnp.zeros_like(low)], axis=0
        ).astype(BF16)


def attend(info, q, own, ahead, behind, far_low, far_high):
    vmem = pl.BlockSpec(memory_space=pltpu.VMEM)
    return pl.pallas_call(
        attend_kernel,
        out_shape=jax.ShapeDtypeStruct((4, OROWS, TOK), BF16),
        in_specs=[pl.BlockSpec(memory_space=pltpu.SMEM)] + [vmem] * 6,
        out_specs=vmem,
        scratch_shapes=[
            pltpu.VMEM((4, TILE, HEAD), BF16),
            pltpu.VMEM((4, VROWS, TILE), BF16),
            pltpu.VMEM((TILE, TOK), F32),
            pltpu.VMEM((TILE, TOK), F32),
            pltpu.VMEM((8, TOK), F32),
            pltpu.VMEM((4, GROUP, VROWS, TOK), F32),
            pltpu.VMEM((4, 8, TOK), F32),
            pltpu.VMEM((TILE, 128), F32),
        ],
        compiler_params=pltpu.CompilerParams(vmem_limit_bytes=40 * 2**20),
        name="attend",
    )(info, q, own, ahead, behind, far_low, far_high)


def combine_kernel(parts, out_ref):
    logs = []
    for y in range(NY):
        tail = parts[y, GROUP * HEAD : OROWS, :].astype(F32)
        logs.append(tail[0:4] + tail[4:8] + tail[8:12])
    best = functools.reduce(jnp.maximum, logs)
    shares = [jnp.exp2(l - best) for l in logs]
    whole = 1.0 / functools.reduce(jnp.add, shares)
    for h in range(GROUP):
        rows = slice(h * HEAD, (h + 1) * HEAD)
        total = None
        for y in range(NY):
            part = parts[y, rows, :].astype(F32) * (shares[y] * whole)[h : h + 1, :]
            total = part if total is None else total + part
        out_ref[:, rows] = total.T.astype(BF16)


def combine(parts):
    vmem = pl.BlockSpec(memory_space=pltpu.VMEM)
    return pl.pallas_call(
        combine_kernel,
        out_shape=jax.ShapeDtypeStruct((TOK, GROUP * HEAD), BF16),
        in_specs=[vmem],
        out_specs=vmem,
        compiler_params=pltpu.CompilerParams(vmem_limit_bytes=16 * 2**20),
        name="combine",
    )(parts)


def pack_kernel(core, weight, out, sems):
    copies = [
        pltpu.make_async_copy(
            weight.at[:, pl.ds(pl.multiple_of((2 * x + 1 - core[0]) * WIDTH, WIDTH), WIDTH)],
            out.at[x],
            sems.at[x],
        )
        for x in range(NX)
    ]
    for copy in copies:
        copy.start()
    for copy in copies:
        copy.wait()


def pack(core, weight):
    anywhere = pl.BlockSpec(memory_space=pl.ANY)
    return pl.pallas_call(
        pack_kernel,
        out_shape=jax.ShapeDtypeStruct((NX, WIDTH, WIDTH), BF16),
        in_specs=[pl.BlockSpec(memory_space=pltpu.SMEM), anywhere],
        out_specs=anywhere,
        scratch_shapes=[pltpu.SemaphoreType.DMA((NX,))],
        name="pack",
    )(core, weight)


def project_kernel(core, both, own_weight, other_weight, out_ref):
    mine, other = both[core[0]], both[1 - core[0]]
    out_ref[0] = (
        dot(mine, own_weight[...], ((1,), (0,))) + dot(other, other_weight[0], ((1,), (0,)))
    ).astype(BF16)


def project(core, both, own_weight, other_weight):
    return pl.pallas_call(
        project_kernel,
        grid_spec=pltpu.PrefetchScalarGridSpec(
            num_scalar_prefetch=1,
            grid=(NX,),
            in_specs=[
                pl.BlockSpec((2, TOK, WIDTH), lambda x, core: (0, 0, 0)),
                pl.BlockSpec((WIDTH, WIDTH), lambda x, core: (0, 2 * x + core[0])),
                pl.BlockSpec((1, WIDTH, WIDTH), lambda x, core: (x, 0, 0)),
            ],
            out_specs=pl.BlockSpec((1, TOK, WIDTH), lambda x, core: (x, 0, 0)),
        ),
        out_shape=jax.ShapeDtypeStruct((NX, TOK, WIDTH), BF16),
        compiler_params=pltpu.CompilerParams(vmem_limit_bytes=16 * 2**20),
        name="project",
    )(core, both, own_weight, other_weight)


def split_ids(block_ids):
    return (block_ids // 32).astype(BF16), (block_ids % 32).astype(BF16)


def local(queries, keys, values, block_ids, out_weight):
    ctx = ("y", "z")
    high, low = split_ids(block_ids)
    info = lax.dynamic_index_in_dim(
        jnp.asarray(schedule()), lax.axis_index(ctx), 0, keepdims=False
    )
    core = lax.axis_index("core").reshape(1)

    q_ids = jnp.zeros((16, GROUP * HEAD), BF16).at[0].set(jnp.concatenate([high, low]))
    q_all = lax.all_gather(jnp.concatenate([queries, q_ids], axis=0), "y", axis=0)
    id_rows = jnp.concatenate([high, low]).reshape(4, 128)
    block = jnp.concatenate([keys, values, id_rows, jnp.zeros((12, 128), BF16)], axis=0)
    own = lax.all_gather(block, ctx, axis=0, axis_index_groups=ring_groups())
    ahead = lax.ppermute(own, ctx, ring_step(1))
    behind = lax.ppermute(own, ctx, ring_step(-1))
    far_low = lax.ppermute(own[0:2], ctx, ring_step(2))
    far_high = lax.ppermute(own[2:4], ctx, ring_step(-2))

    weight, own = lax.optimization_barrier((out_weight, own))
    other_weight = lax.ppermute(pack(core, weight), "core", [(0, 1), (1, 0)])

    partial = attend(info, q_all, own, ahead, behind, far_low, far_high)
    partial = lax.all_to_all(partial, "y", 0, 0, tiled=True)
    both = lax.all_gather(combine(partial), "core", axis=0)
    share = project(core, both, out_weight, other_weight)
    shares = lax.all_to_all(share, "x", 0, 0, tiled=True)
    return jnp.sum(shares.astype(F32), axis=0).astype(BF16)


def solution(mesh):
    grid = Mesh(mesh.devices.reshape(NY, NZ, NX, 2), ("y", "z", "x", "core"))
    ctx, head = ("y", "z"), ("x", "core")
    return jax.shard_map(
        local,
        mesh=grid,
        in_specs=(P(ctx, head), P(ctx, head), P(ctx, head), P(ctx), P(head, None)),
        out_specs=P(ctx, head),
        check_vma=False,
    )
```

time: 724 us -> 216 us (0.30)
  waiting for transfers between devices: 358 us -> 15.4 us
  loops' own time: 163 us -> 0 us
  Pallas kernels: 0 us -> 81.3 us
  local copies, waits for them, and re-layouts: 59.2 us -> 4.64 us
  other arithmetic: 43.9 us -> 3.31 us
  starting transfers between devices: 0.08 us -> 19.7 us
    all_gather x2 -> x1, waiting for transfers between devices: 213 us -> 0.02 us  [local(): lax.all_gather(jnp.concatenate([queries, q_ids], axis=0), 'y', axis=0)]
    another operation x129 -> x0, loops' own time: 163 us -> none  [the longest x1 160 us: local(): lax.scan(one_block, carry, (key_blocks, value_blocks, id_blocks))]
    reduce_scatter x1 -> x0, waiting for transfers between devices: 143 us -> none  [local(): lax.psum_scatter(partial_value.astype(jnp.bfloat16), 'head', scatter_dime...]
    pallas_call x0 -> x4, Pallas kernels: none -> 81.3 us  [the longest x1 64.7 us: pack(): pl.pallas_call(pack_kernel, out_shape=jax.ShapeDtypeStruct((NX, WIDTH, WI...]
    squeeze x64 -> x1, local copies, waits for them, and re-layouts: 56.7 us -> 0.7 us  [local(): lax.dynamic_index_in_dim(jnp.asarray(schedule()), lax.axis_index(ctx), 0,...]
    reduce_min x64 -> x0, other arithmetic: 41.8 us -> none  [one_block(): jnp.min(key_ids) > jnp.max(query_ids)]
    all_to_all x0 -> x2, blocking collectives: none -> 35.1 us  [the longest x1 18.1 us: local(): shares = lax.all_to_all(share, 'x', 0, 0, tiled=True)]
    all_gather x1 -> x2, blocking collectives: 73.9 us -> 41.2 us  [the longest x1 37.4 us: local(): own = lax.all_gather(block, ctx, axis=0, axis_index_groups=ring_groups())]
  transfers between devices with their start and end apart: 3 -> 6, of which waited for: 3 -> 1; matrix products, arithmetic and copies ran while one was open for 0% -> 2% of each run, Pallas kernels for 0% -> 37%
where the time goes in v1:
time: 216 us; the launch traced here: 214 us
  Pallas kernels  81.3 us (38%)
  blocking collectives  76.3 us (35%)
  starting transfers between devices  19.7 us (9%)
  waiting for transfers between devices  15.4 us (7%)
  between operations  13.5 us (6%)
  local copies, waits for them, and re-layouts  4.64 us (2%)
  other arithmetic  3.31 us (2%)
    pallas_call x1, Pallas kernels, pack(): pl.pallas_call(pack_kernel, out_shape=jax.ShapeDtypeStruct((NX, WIDTH, WI...  64.7 us
    all_gather x1, blocking collectives, local(): own = lax.all_gather(block, ctx, axis=0, axis_index_groups=ring_groups())  37.4 us
    all_to_all x1, blocking collectives, local(): shares = lax.all_to_all(share, 'x', 0, 0, tiled=True)  18.1 us
    all_to_all x1, blocking collectives, local(): partial = lax.all_to_all(partial, 'y', 0, 0, tiled=True)  17 us
    ppermute x1, waiting for transfers between devices, local(): far_low = lax.ppermute(own[0:2], ctx, ring_step(2))  15.3 us
    pallas_call x1, Pallas kernels, attend(): pl.pallas_call(attend_kernel, out_shape=jax.ShapeDtypeStruct((4, OROWS, T...  14.3 us
    ppermute x1, starting transfers between devices, local(): ahead = lax.ppermute(own, ctx, ring_step(1))  6.68 us
    ppermute x1, starting transfers between devices, local(): other_weight = lax.ppermute(pack(core, weight), 'core', [(0, 1), (1, 0)])  4.89 us
  transfers between devices with their start and end apart: 6, of which 1 were waited for; matrix products, arithmetic and copies ran while one was open for 2% of the time, Pallas kernels for 37%

profile of v1, /device:TPU:1, one launch (start us, length us, event | category | flops | bytes accessed | tf_op | source)
XLA Modules:
  0.0 214.1 jit_solution(10384955119020505965)
XLA Ops:
  6.5 0.7 fusion.3
  7.2 1.7 fusion.1
  9.0 0.0 all-gather.5.cloned.1.call-update
  9.0 1.8 concatenate.22
  10.8 37.4 %all-gather.1 = bf16[2112,128]{1,0:T(8,128)(2,1)S(1)} all-gather(bf16[528,128]{1,0:T(8,128)(2,1)S(1)} %concatenate.22), channel_id=3, replica_groups={{0,160,320,480},{8,168,328,488},{16,176,336,496},{24,184,344,504},{32,1..., dimensions={0}, use_global_device_ids=true | all-gather | bytes 675840 | tf_op jit(solution)/shard_map/all_gather | solution.py:317
  48.2 64.7 %pack.1 = bf16[4,512,512]{2,1,0:T(8,128)(2,1)} custom-call(s32[1]{0:T(128)} %bitcast.core, bf16[512,4096]{1,0:T(8,128)(2,1)} %own_weight.1), custom_call_target="tpu_custom_call" | custom-call | tf_op jit(solution)/shard_map/pack/pallas_call | solution.py:265
  112.9 4.9 %collective-permute-start.4 = (bf16[4,512,512]{2,1,0:T(8,128)(2,1)}, bf16[4,512,512]{2,1,0:T(8,128)(2,1)S(1)}, u32[]{:S(2)}, u32[]{:S(2)}) collective-permute-start(bf16[4,512,512]{2,1,0:T(8,128)(2,1)} %pack.1), channel_id=1, source_target_pairs={{0,1},{1,0},{2,3},{3,2},{4,5},{5,4},{6,7},{7,6},{8,9},{9,8},{10,11... | collective-permute-start | bytes 6291464 | tf_op jit(solution)/shard_map/ppermute | solution.py:324
  117.8 1.9 collective-permute-start.1
  119.7 6.7 %collective-permute-start = (bf16[4,528,128]{2,1,0:T(8,128)(2,1)S(1)}, bf16[4,528,128]{2,1,0:T(8,128)(2,1)}, u32[]{:S(2)}, u32[]{:S(2)}) collective-permute-start(bf16[4,528,128]{2,1,0:T(8,128)(2,1)S(1)} %bitcast.11), channel_id=1, source_target_pairs={{8,0},{16,8},{24,16},{160,24},{168,160},{176,168},{184,176},{320,1... | collective-permute-start | bytes 1622024 | tf_op jit(solution)/shard_map/ppermute | solution.py:318
  126.4 0.8 fusion.4
  127.3 1.9 collective-permute-start.2
  129.2 4.3 %collective-permute-start.3 = (bf16[2,528,128]{2,1,0:T(8,128)(2,1)}, bf16[2,528,128]{2,1,0:T(8,128)(2,1)}, u32[]{:S(2)}, u32[]{:S(2)}) collective-permute-start(bf16[2,528,128]{2,1,0:T(8,128)(2,1)} %bitcast.7), channel_id=1, source_target_pairs={{496,0},{504,8},{0,16},{8,24},{16,160},{24,168},{160,176},{168,184... | collective-permute-start | bytes 811016 | tf_op jit(solution)/shard_map/ppermute | solution.py:321
  133.4 0.7 dynamic-slice_bitcast_fusion.info
  134.1 15.3 %collective-permute-done.2.far_low = bf16[2,528,128]{2,1,0:T(8,128)(2,1)S(1)} collective-permute-done((bf16[2,528,128]{2,1,0:T(8,128)(2,1)}, bf16[2,528,128]{2,1,0:T(8,128)(2,1)S(1)}, u32[]{:S(2)}, u32[]{:S(2)}) %collective-permute-start.2) | collective-permute-done | bytes 270368 | tf_op jit(solution)/shard_map/ppermute | solution.py:320
  149.5 0.0 all-gather.5.cloned.1.call-done
  149.5 1.2 copy-done.1
  150.7 14.3 %attend.1 = bf16[4,528,256]{2,1,0:T(8,128)(2,1)S(1)} custom-call(s32[32]{0:T(128)S(1)} %dynamic-slice_bitcast_fusion.info, bf16[4,272,512]{2,1,0:T(8,128)(2,1)S(1)} %bitcast.14, bf16[4,528,128]{2,1,0:T(8,128)(2,1)S(1)} %bitcast.12, bf16[4,528,128]{2,1,0:T(8,128)(2,1)} %collective-permute-done.ahead, bf16[4,528,128]{2,1,0:T(8,128)(2,1)S(1)} %collective-permute-done.1.behind, ...), custom_call_target="tpu_custom_call" | custom-call | tf_op jit(solution)/shard_map/attend/pallas_call | solution.py:199
  165.1 0.0 copy-start
  165.1 17.0 %all_to_all.10.parts = bf16[4,528,256]{2,1,0:T(8,128)(2,1)S(1)} all-to-all(bf16[4,528,256]{2,1,0:T(8,128)(2,1)S(1)} %attend.1), channel_id=1, replica_groups=mesh['y'=4,'z'=16,'x'=4,'core'=2] {'y'}, dimensions={0} | all-to-all | bytes 2162688 | tf_op jit(solution)/shard_map/all_to_all | solution.py:327
  182.1 0.3 combine.1
  182.4 3.8 %all-gather.2 = bf16[512,512]{1,0:T(8,128)(2,1)S(1)} all-gather(bf16[256,512]{1,0:T(8,128)(2,1)S(1)} %combine.1), channel_id=4, replica_groups=mesh['y'=4,'z'=16,'x'=4,'core'=2] {'core'}, dimensions={0}, use_global_device_ids=true | all-gather | bytes 786432 | tf_op jit(solution)/shard_map/all_gather | solution.py:328
  186.3 2.0 project.1
  188.3 18.1 %all_to_all.11 = bf16[4,256,512]{2,1,0:T(8,128)(2,1)S(1)} all-to-all(bf16[4,256,512]{2,1,0:T(8,128)(2,1)S(1)} %project.1), channel_id=1, replica_groups=mesh['y'=4,'z'=16,'x'=4,'core'=2] {'x'}, dimensions={0} | all-to-all | bytes 2097152 | tf_op jit(solution)/shard_map/all_to_all | solution.py:330
  206.3 0.9 reduce_sum.12
  (10 shorter events, 0.0 us)
Async XLA Ops:
  6.5 143.0 %all-gather.5.cloned.1.call-start = ((), (), s32[]{:S(2)}) async-start(), calls=%async_computation.2 | async-start | bytes 1392640 | tf_op jit(solution)/shard_map/all_gather | solution.py:314
  112.9 73.4 %collective-permute-start.4 = (bf16[4,512,512]{2,1,0:T(8,128)(2,1)}, bf16[4,512,512]{2,1,0:T(8,128)(2,1)S(1)}, u32[]{:S(2)}, u32[]{:S(2)}) collective-permute-start(bf16[4,512,512]{2,1,0:T(8,128)(2,1)} %pack.1), channel_id=1, source_target_pairs={{0,1},{1,0},{2,3},{3,2},{4,5},{5,4},{6,7},{7,6},{8,9},{9,8},{10,11... | collective-permute-start | bytes 6291464 | tf_op jit(solution)/shard_map/ppermute | solution.py:324
  117.8 31.7 %collective-permute-start.1 = (bf16[4,528,128]{2,1,0:T(8,128)(2,1)S(1)}, bf16[4,528,128]{2,1,0:T(8,128)(2,1)S(1)}, u32[]{:S(2)}, u32[]{:S(2)}) collective-permute-start(bf16[4,528,128]{2,1,0:T(8,128)(2,1)S(1)} %bitcast.10), channel_id=1, source_target_pairs={{504,0},{0,8},{8,16},{16,24},{24,160},{160,168},{168,176},{176,184... | collective-permute-start | bytes 1622024 | tf_op jit(solution)/shard_map/ppermute | solution.py:319
  119.7 29.7 %collective-permute-start = (bf16[4,528,128]{2,1,0:T(8,128)(2,1)S(1)}, bf16[4,528,128]{2,1,0:T(8,128)(2,1)}, u32[]{:S(2)}, u32[]{:S(2)}) collective-permute-start(bf16[4,528,128]{2,1,0:T(8,128)(2,1)S(1)} %bitcast.11), channel_id=1, source_target_pairs={{8,0},{16,8},{24,16},{160,24},{168,160},{176,168},{184,176},{320,1... | collective-permute-start | bytes 1622024 | tf_op jit(solution)/shard_map/ppermute | solution.py:318
  127.3 22.2 %collective-permute-start.2 = (bf16[2,528,128]{2,1,0:T(8,128)(2,1)}, bf16[2,528,128]{2,1,0:T(8,128)(2,1)S(1)}, u32[]{:S(2)}, u32[]{:S(2)}) collective-permute-start(bf16[2,528,128]{2,1,0:T(8,128)(2,1)} %bitcast.6), channel_id=1, source_target_pairs={{16,0},{24,8},{160,16},{168,24},{176,160},{184,168},{320,176},{328... | collective-permute-start | bytes 811016 | tf_op jit(solution)/shard_map/ppermute | solution.py:320
  129.2 20.3 %collective-permute-start.3 = (bf16[2,528,128]{2,1,0:T(8,128)(2,1)}, bf16[2,528,128]{2,1,0:T(8,128)(2,1)}, u32[]{:S(2)}, u32[]{:S(2)}) collective-permute-start(bf16[2,528,128]{2,1,0:T(8,128)(2,1)} %bitcast.7), channel_id=1, source_target_pairs={{496,0},{504,8},{0,16},{8,24},{16,160},{24,168},{160,176},{168,184... | collective-permute-start | bytes 811016 | tf_op jit(solution)/shard_map/ppermute | solution.py:321
  149.5 1.2 copy-start.1
  165.1 21.2 %copy-start = (bf16[512,4096]{1,0:T(8,128)(2,1)S(1)}, bf16[512,4096]{1,0:T(8,128)(2,1)}, u32[]{:S(2)}) copy-start(bf16[512,4096]{1,0:T(8,128)(2,1)} %own_weight.1) | copy-start | bytes 12582916
Sparse Core Ops, SparseCore 0:
  9.5 37.7 all-gather.4

commit v2 on v1

v2 whole, which is shorter than its diff:
```python
import functools

import jax
import jax.numpy as jnp
import numpy as np
from jax import lax
from jax.experimental import pallas as pl
from jax.experimental.pallas import tpu as pltpu
from jax.sharding import Mesh
from jax.sharding import PartitionSpec as P

HEAD = 128
GROUP = 4
TOK = 256
LOG_SCALE = float(128**-0.5 * np.log2(np.e))
HIDDEN = -1e30
FLOOR = -1e29
ROWS = TOK * 2 + 16
QROWS = TOK + 16
OROWS = GROUP * HEAD + 16
VROWS = HEAD + 16
WIDTH = GROUP * HEAD
F32, BF16 = jnp.float32, jnp.bfloat16
NX, NY, NZ = 4, 4, 16


def ring_place(d, z):
    return ((z // 4 - d) % NY) * NZ + z


def ring_step(step):
    return [
        (ring_place(d, (z + step) % NZ), ring_place(d, z)) for d in range(4) for z in range(NZ)
    ]


def ring_groups():
    return [
        [i * NZ + ((i + d) % 4) * 4 + zl for i in range(4)] for d in range(4) for zl in range(4)
    ]


def run_on():
    table = np.zeros((NY * NZ, 8), np.int32)
    for y in range(NY - 1):
        table[y * NZ + NZ - 1, 0:3] = 1, y, y + 1
    return table


def dot(a, b, dims):
    return lax.dot_general(a, b, (dims, ((), ())), preferred_element_type=F32)


def attend_kernel(kinds, first, last, info, q_ref, *refs):
    n_blocks = 1 + max(operand for kind in kinds for operand, _ in kind)
    blocks, refs = refs[:n_blocks], refs[n_blocks:]
    if first:
        acc_in = max_in = None
    else:
        acc_in, max_in, *refs = refs
    if last:
        out_ref, acc, row_max, *refs = refs
    else:
        acc, row_max, *refs = refs
    v_buf, even, odd, top, ids = refs
    scores = (even, odd)

    def key_block(n, i):
        operand, index = kinds[n][i]
        return blocks[operand].at[index]

    for n in range(len(kinds)):
        for i in range(4):
            block = key_block(n, i)
            v_buf[n, i, 0:HEAD, :] = block[TOK : 2 * TOK, :].T
            v_buf[n, i, HEAD:VROWS, :] = jnp.ones((16, TOK), BF16)
            rows = block[2 * TOK : 2 * TOK + 16, :].astype(F32)
            for half in range(2):
                line = rows[half : half + 1, :] * 32.0 + rows[half + 2 : half + 3, :]
                ids[n, i, half * 128 : half * 128 + 128, :] = jnp.broadcast_to(line, (128, 128)).T

    def query(q, h):
        return q_ref[q, 0:TOK, pl.ds(pl.multiple_of(h * HEAD, HEAD), HEAD)]

    def query_ids(q):
        tail = q_ref[q, TOK : TOK + 16, :].astype(F32)
        return (tail[:, 0:TOK] * 32.0 + tail[:, TOK : 2 * TOK])[0:1, :]

    def hide(s, q, n, i):
        seen = jnp.concatenate([ids[n, i], ids[n, i]], axis=1) <= query_ids(q)
        return jnp.where(seen, s, HIDDEN)

    def score(q, h, n, i):
        s = dot(key_block(n, i)[0:TOK, :], query(q, h), ((1,), (1,)))
        return hide(s, q, n, i) if i == q else s

    def fold(s):
        return jnp.max(s.reshape(TOK // 8, 8, TOK), axis=0)

    parts = [[(n, i) for i in range(q + 1) for n in range(len(kinds))] for q in range(4)]

    def score_into(q, h, at, best):
        s = score(q, h, *parts[q][at])
        scores[q % 2][at * TOK : (at + 1) * TOK, :] = s
        return fold(s) if best is None else jnp.maximum(best, fold(s))

    best = None
    for at in range(len(parts[0])):
        best = score_into(0, 0, at, best)
    top[...] = best

    def head(h, carry):
        for q in range(4):
            q_next, h_next = (q + 1, h) if q < 3 else (0, jnp.minimum(h + 1, GROUP - 1))
            peak = jnp.max(top[...], axis=0, keepdims=True)
            if first:
                new = jnp.maximum(peak, FLOOR)
                total = None
            else:
                old = max_in[q, h]
                new = jnp.maximum(old, peak)
                total = acc_in[q, h] * jnp.exp2((old - new) * LOG_SCALE)
            row_max[q, h] = new
            best = None
            here, there = len(parts[q]), len(parts[q_next])
            done = 0
            for at, (n, i) in enumerate(parts[q]):
                until = (at + 1) * there // here
                for other in range(done, until):
                    best = score_into(q_next, h_next, other, best)
                done = until
                weights = jnp.exp2(
                    (scores[q % 2][at * TOK : (at + 1) * TOK, :] - new) * LOG_SCALE
                ).astype(BF16)
                part = dot(v_buf[n, i], weights, ((1,), (0,)))
                total = part if total is None else total + part
            acc[q, h] = total
            top[...] = best
        return carry

    lax.fori_loop(0, GROUP, head, 0)

    if kinds == AHEAD_BEHIND:
        @pl.when(info[0] == 1)
        def _():
            q, i = info[1], info[2]
            block = blocks[0].at[i]
            seen = jnp.concatenate([ids[0, i], ids[0, i]], axis=1) <= query_ids(q)
            for h in range(GROUP):
                s = dot(block[0:TOK, :], query(q, h), ((1,), (1,)))
                s = jnp.where(seen, s, HIDDEN)
                old = row_max[q, h]
                new = jnp.maximum(old, jnp.max(s, axis=0, keepdims=True))
                weights = jnp.exp2((s - new) * LOG_SCALE).astype(BF16)
                acc[q, h] = acc[q, h] * jnp.exp2((old - new) * LOG_SCALE) + dot(
                    v_buf[0, i], weights, ((1,), (0,))
                )
                row_max[q, h] = new

    if last:
        for q in range(4):
            sums = []
            for h in range(GROUP):
                total = jnp.maximum(acc[q, h, HEAD : HEAD + 1, :], 0.5)
                out_ref[q, h * HEAD : (h + 1) * HEAD, :] = (
                    acc[q, h, 0:HEAD, :] * (1.0 / total)
                ).astype(BF16)
                sums.append(row_max[q, h] * LOG_SCALE + jnp.log2(total))
            log_sum = jnp.concatenate(sums, axis=0)
            high = log_sum.astype(BF16).astype(F32)
            mid = (log_sum - high).astype(BF16).astype(F32)
            low = log_sum - high - mid
            out_ref[q, GROUP * HEAD : OROWS, :] = jnp.concatenate(
                [high, mid, low, jnp.zeros_like(low)], axis=0
            ).astype(BF16)


OWN = (((0, 0), (0, 1), (0, 2), (0, 3)),)
AHEAD_BEHIND = (((0, 0), (0, 1), (0, 2), (0, 3)), ((1, 0), (1, 1), (1, 2), (1, 3)))
FAR = (((0, 0), (0, 1), (1, 0), (1, 1)),)


def attend(kinds, first, last, info, q, blocks, state):
    vmem = pl.BlockSpec(memory_space=pltpu.VMEM)
    n = len(kinds)
    acc = jax.ShapeDtypeStruct((4, GROUP, VROWS, TOK), F32)
    row_max = jax.ShapeDtypeStruct((4, GROUP, 1, TOK), F32)
    running = [pltpu.VMEM(acc.shape, F32), pltpu.VMEM(row_max.shape, F32)]
    scores = 10 * n * 4 * TOK * TOK
    return pl.pallas_call(
        functools.partial(attend_kernel, kinds, first, last),
        out_shape=jax.ShapeDtypeStruct((4, OROWS, TOK), BF16) if last else (acc, row_max),
        in_specs=[pl.BlockSpec(memory_space=pltpu.SMEM)] + [vmem] * (1 + len(blocks) + len(state)),
        out_specs=vmem if last else (vmem, vmem),
        scratch_shapes=(running if last else [])
        + [
            pltpu.VMEM((n, 4, VROWS, TOK), BF16),
            pltpu.VMEM((3 * n * TOK, TOK), F32),
            pltpu.VMEM((4 * n * TOK, TOK), F32),
            pltpu.VMEM((8, TOK), F32),
            pltpu.VMEM((n, 4, TOK, 128), F32),
        ],
        compiler_params=pltpu.CompilerParams(vmem_limit_bytes=32 * 2**20),
        cost_estimate=pl.CostEstimate(
            flops=scores * 8 * HEAD, transcendentals=scores, bytes_accessed=6 * 2**20
        ),
        name="attend",
    )(info, q, *blocks, *state)


def combine_kernel(parts, out_ref):
    logs = []
    for y in range(NY):
        tail = parts[y, GROUP * HEAD : OROWS, :].astype(F32)
        logs.append(tail[0:4] + tail[4:8] + tail[8:12])
    best = functools.reduce(jnp.maximum, logs)
    shares = [jnp.exp2(l - best) for l in logs]
    whole = 1.0 / functools.reduce(jnp.add, shares)
    for h in range(GROUP):
        rows = slice(h * HEAD, (h + 1) * HEAD)
        total = None
        for y in range(NY):
            part = parts[y, rows, :].astype(F32) * (shares[y] * whole)[h : h + 1, :]
            total = part if total is None else total + part
        out_ref[:, rows] = total.T.astype(BF16)


def combine(parts):
    vmem = pl.BlockSpec(memory_space=pltpu.VMEM)
    return pl.pallas_call(
        combine_kernel,
        out_shape=jax.ShapeDtypeStruct((TOK, GROUP * HEAD), BF16),
        in_specs=[vmem],
        out_specs=vmem,
        compiler_params=pltpu.CompilerParams(vmem_limit_bytes=16 * 2**20),
        name="combine",
    )(parts)


def pack_kernel(core, weight, out):
    out[0] = weight[...]


def pack(core, weight):
    return pl.pallas_call(
        pack_kernel,
        grid_spec=pltpu.PrefetchScalarGridSpec(
            num_scalar_prefetch=1,
            grid=(NX,),
            in_specs=[pl.BlockSpec((WIDTH, WIDTH), lambda x, core: (0, 2 * x + 1 - core[0]))],
            out_specs=pl.BlockSpec((1, WIDTH, WIDTH), lambda x, core: (x, 0, 0)),
        ),
        out_shape=jax.ShapeDtypeStruct((NX, WIDTH, WIDTH), BF16),
        compiler_params=pltpu.CompilerParams(vmem_limit_bytes=16 * 2**20),
        name="pack",
    )(core, weight)


def project_kernel(core, both, own_weight, other_weight, out_ref):
    mine, other = both[core[0]], both[1 - core[0]]
    out_ref[0] = (
        dot(mine, own_weight[...], ((1,), (0,))) + dot(other, other_weight[0], ((1,), (0,)))
    ).astype(BF16)


def project(core, both, own_weight, other_weight):
    return pl.pallas_call(
        project_kernel,
        grid_spec=pltpu.PrefetchScalarGridSpec(
            num_scalar_prefetch=1,
            grid=(NX,),
            in_specs=[
                pl.BlockSpec((2, TOK, WIDTH), lambda x, core: (0, 0, 0)),
                pl.BlockSpec((WIDTH, WIDTH), lambda x, core: (0, 2 * x + core[0])),
                pl.BlockSpec((1, WIDTH, WIDTH), lambda x, core: (x, 0, 0)),
            ],
            out_specs=pl.BlockSpec((1, TOK, WIDTH), lambda x, core: (x, 0, 0)),
        ),
        out_shape=jax.ShapeDtypeStruct((NX, TOK, WIDTH), BF16),
        compiler_params=pltpu.CompilerParams(vmem_limit_bytes=16 * 2**20),
        name="project",
    )(core, both, own_weight, other_weight)


def split_ids(block_ids):
    return (block_ids // 32).astype(BF16), (block_ids % 32).astype(BF16)


def local(queries, keys, values, block_ids, out_weight):
    ctx = ("y", "z")
    high, low = split_ids(block_ids)
    info = lax.dynamic_index_in_dim(
        jnp.asarray(run_on()), lax.axis_index(ctx), 0, keepdims=False
    )
    core = lax.axis_index("core").reshape(1)

    q_ids = jnp.zeros((16, GROUP * HEAD), BF16).at[0].set(jnp.concatenate([high, low]))
    q_all = lax.all_gather(jnp.concatenate([queries, q_ids], axis=0), "y", axis=0)
    id_rows = jnp.concatenate([high, low]).reshape(4, 128)
    block = jnp.concatenate([keys, values, id_rows, jnp.zeros((12, 128), BF16)], axis=0)
    own = lax.all_gather(block, ctx, axis=0, axis_index_groups=ring_groups())
    ahead = lax.ppermute(own, ctx, ring_step(1))
    behind = lax.ppermute(own, ctx, ring_step(-1))
    far_low = lax.ppermute(own[0:2], ctx, ring_step(2))
    far_high = lax.ppermute(own[2:4], ctx, ring_step(-2))

    state = attend(OWN, True, False, info, q_all, [own], ())
    weight, state = lax.optimization_barrier((out_weight, state))
    other_weight = lax.ppermute(pack(core, weight), "core", [(0, 1), (1, 0)])
    state = attend(AHEAD_BEHIND, False, False, info, q_all, [ahead, behind], state)
    partial = attend(FAR, False, True, info, q_all, [far_low, far_high], state)
    partial = lax.all_to_all(partial, "y", 0, 0, tiled=True)
    both = lax.all_gather(combine(partial), "core", axis=0)
    share = project(core, both, out_weight, other_weight)
    shares = lax.all_to_all(share, "x", 0, 0, tiled=True)
    return jnp.sum(shares.astype(F32), axis=0).astype(BF16)


def solution(mesh):
    grid = Mesh(mesh.devices.reshape(NY, NZ, NX, 2), ("y", "z", "x", "core"))
    ctx, head = ("y", "z"), ("x", "core")
    return jax.shard_map(
        local,
        mesh=grid,
        in_specs=(P(ctx, head), P(ctx, head), P(ctx, head), P(ctx), P(head, None)),
        out_specs=P(ctx, head),
        check_vma=False,
    )
```

time: 216 us -> 145 us (0.67)
  Pallas kernels: 81.3 us -> 24.1 us
  waiting for transfers between devices: 15.4 us -> 6.92 us
  starting transfers between devices: 19.7 us -> 16.9 us
    pallas_call x2 -> x4, Pallas kernels: 79 us -> 21.8 us  [the longest x3 21.4 us: attend(): pl.pallas_call(functools.partial(attend_kernel, kinds, first, last), out_...]
    ppermute x1, waiting for transfers between devices: 15.3 us -> 0.01 us  [local(): far_low = lax.ppermute(own[0:2], ctx, ring_step(2))]
    ppermute x1, waiting for transfers between devices: 0.01 us -> 6.89 us  [local(): far_high = lax.ppermute(own[2:4], ctx, ring_step(-2))]
  transfers between devices with their start and end apart: 6 -> 6, of which waited for: 1 -> 1; matrix products, arithmetic and copies ran while one was open for 2% -> 2% of each run, Pallas kernels for 37% -> 15%
where the time goes in v2:
time: 145 us
  blocking collectives  76 us (52%)
  Pallas kernels  24.1 us (17%)
  starting transfers between devices  16.9 us (12%)
  between operations  13.5 us (9%)
  waiting for transfers between devices  6.92 us (5%)
  local copies, waits for them, and re-layouts  3.84 us (3%)
  other arithmetic  3.3 us (2%)
    all_gather x1, blocking collectives, local(): own = lax.all_gather(block, ctx, axis=0, axis_index_groups=ring_groups())  37.4 us
    pallas_call x3, Pallas kernels, attend(): pl.pallas_call(functools.partial(attend_kernel, kinds, first, last), out_...  21.4 us
    all_to_all x1, blocking collectives, local(): shares = lax.all_to_all(share, 'x', 0, 0, tiled=True)  18.1 us
    all_to_all x1, blocking collectives, local(): partial = lax.all_to_all(partial, 'y', 0, 0, tiled=True)  16.7 us
    ppermute x1, waiting for transfers between devices, local(): far_high = lax.ppermute(own[2:4], ctx, ring_step(-2))  6.89 us
    ppermute x1, starting transfers between devices, local(): ahead = lax.ppermute(own, ctx, ring_step(1))  5.28 us
    all_gather x1, blocking collectives, local(): both = lax.all_gather(combine(partial), 'core', axis=0)  3.89 us
    ppermute x1, starting transfers between devices, local(): other_weight = lax.ppermute(pack(core, weight), 'core', [(0, 1), (1, 0)])  3.51 us
  transfers between devices with their start and end apart: 6, of which 1 were waited for; matrix products, arithmetic and copies ran while one was open for 2% of the time, Pallas kernels for 15%

profile of v2, /device:TPU:1, one launch (start us, length us, event | category | flops | bytes accessed | tf_op | source)
XLA Modules:
  0.0 144.6 jit_solution(132197409097295970)
XLA Ops:
  6.5 0.7 fusion.3
  7.2 1.7 %fusion.1 = bf16[272,512]{1,0:T(8,128)(2,1)} fusion(bf16[1,512]{1,0:T(2,128)(2,1)S(1)} %reshape.35, bf16[256,512]{1,0:T(8,128)(2,1)} %param.8), kind=kLoop, calls=%fused_computation.2 | loop fusion | flops 835584 | bytes 541696 | tf_op jit(solution)/shard_map/concatenate | solution.py:298
  8.9 0.0 all-gather.5.cloned.1.call-update
  9.0 1.8 %concatenate.22 = bf16[528,128]{1,0:T(8,128)(2,1)S(1)} concatenate(bf16[256,128]{1,0:T(8,128)(2,1)} %param.9, bf16[256,128]{1,0:T(8,128)(2,1)} %param.10, bf16[2,128]{1,0:T(2,128)(2,1)S(1)} %bitcast.19, bf16[2,128]{1,0:T(2,128)(2,1)S(1)} %bitcast.20, bf16[12,128]{1,0:T(8,128)(2,1)S(1)} %broadcast_in_dim.4), dimensions={0} | concatenate | bytes 270336 | tf_op jit(solution)/shard_map/concatenate | solution.py:300
  10.8 37.4 %all-gather.1 = bf16[2112,128]{1,0:T(8,128)(2,1)S(1)} all-gather(bf16[528,128]{1,0:T(8,128)(2,1)S(1)} %concatenate.22), channel_id=3, replica_groups={{0,160,320,480},{8,168,328,488},{16,176,336,496},{24,184,344,504},{32,1..., dimensions={0}, use_global_device_ids=true | all-gather | bytes 675840 | tf_op jit(solution)/shard_map/all_gather | solution.py:301
  48.2 5.3 %collective-permute-start.2 = (bf16[4,528,128]{2,1,0:T(8,128)(2,1)S(1)}, bf16[4,528,128]{2,1,0:T(8,128)(2,1)S(1)}, u32[]{:S(2)}, u32[]{:S(2)}) collective-permute-start(bf16[4,528,128]{2,1,0:T(8,128)(2,1)S(1)} %bitcast.10), channel_id=1, source_target_pairs={{8,0},{16,8},{24,16},{160,24},{168,160},{176,168},{184,176},{320,1... | collective-permute-start | bytes 1622024 | tf_op jit(solution)/shard_map/ppermute | solution.py:302
  53.5 1.9 %collective-permute-start.3 = (bf16[4,528,128]{2,1,0:T(8,128)(2,1)S(1)}, bf16[4,528,128]{2,1,0:T(8,128)(2,1)S(1)}, u32[]{:S(2)}, u32[]{:S(2)}) collective-permute-start(bf16[4,528,128]{2,1,0:T(8,128)(2,1)S(1)} %bitcast.11), channel_id=1, source_target_pairs={{504,0},{0,8},{8,16},{16,24},{24,160},{160,168},{168,176},{176,184... | collective-permute-start | bytes 1622024 | tf_op jit(solution)/shard_map/ppermute | solution.py:303
  55.4 0.7 dynamic-slice_bitcast_fusion.info
  56.1 1.2 copy-done.1
  57.4 5.5 %attend.3 = (f32[4,4,144,256]{3,2,1,0:T(8,128)S(1)}, f32[4,4,1,256]{3,2,1,0:T(1,128)S(1)}) custom-call(s32[8]{0:T(128)S(1)} %dynamic-slice_bitcast_fusion.info, bf16[4,272,512]{2,1,0:T(8,128)(2,1)S(1)} %bitcast.14, bf16[4,528,128]{2,1,0:T(8,128)(2,1)S(1)} %bitcast.12), custom_call_target="tpu_custom_call" | custom-call | flops 2684354560 | bytes 6291456 | tf_op jit(solution)/shard_map/attend/pallas_call | solution.py:190
  62.9 0.4 pack.1
  63.3 3.5 %collective-permute-start.4 = (bf16[4,512,512]{2,1,0:T(8,128)(2,1)S(1)}, bf16[4,512,512]{2,1,0:T(8,128)(2,1)S(1)}, u32[]{:S(2)}, u32[]{:S(2)}) collective-permute-start(bf16[4,512,512]{2,1,0:T(8,128)(2,1)S(1)} %pack.1), channel_id=1, source_target_pairs={{0,1},{1,0},{2,3},{3,2},{4,5},{5,4},{6,7},{7,6},{8,9},{9,8},{10,11... | collective-permute-start | bytes 6291464 | tf_op jit(solution)/shard_map/ppermute | solution.py:309
  66.9 3.0 %collective-permute-start = (bf16[2,528,128]{2,1,0:T(8,128)(2,1)S(1)}, bf16[2,528,128]{2,1,0:T(8,128)(2,1)S(1)}, u32[]{:S(2)}, u32[]{:S(2)}) collective-permute-start(bf16[2,528,128]{2,1,0:T(8,128)(2,1)S(1)} %bitcast.18), channel_id=1, source_target_pairs={{16,0},{24,8},{160,16},{168,24},{176,160},{184,168},{320,176},{328... | collective-permute-start | bytes 811016 | tf_op jit(solution)/shard_map/ppermute | solution.py:304
  69.8 3.2 %collective-permute-start.1 = (bf16[2,528,128]{2,1,0:T(8,128)(2,1)S(1)}, bf16[2,528,128]{2,1,0:T(8,128)(2,1)S(1)}, u32[]{:S(2)}, u32[]{:S(2)}) collective-permute-start(bf16[2,528,128]{2,1,0:T(8,128)(2,1)S(1)} %bitcast.17), channel_id=1, source_target_pairs={{496,0},{504,8},{0,16},{8,24},{16,160},{24,168},{160,176},{168,184... | collective-permute-start | bytes 811016 | tf_op jit(solution)/shard_map/ppermute | solution.py:305
  73.1 0.0 collective-permute-done.2.refs_0_
  73.1 9.6 %attend.4 = (f32[4,4,144,256]{3,2,1,0:T(8,128)S(1)}, f32[4,4,1,256]{3,2,1,0:T(1,128)S(1)}) custom-call(s32[8]{0:T(128)S(1)} %dynamic-slice_bitcast_fusion.info, bf16[4,272,512]{2,1,0:T(8,128)(2,1)S(1)} %bitcast.15, bf16[4,528,128]{2,1,0:T(8,128)(2,1)S(1)} %collective-permute-done.2.refs_0_, bf16[4,528,128]{2,1,0:T(8,128)(2,1)S(1)} %collective-permute-done.3.refs_1_, ...), custom_call_target="tpu_custom_call" | custom-call | flops 5368709120 | bytes 6291456 | tf_op jit(solution)/shard_map/attend/pallas_call | solution.py:190
  82.7 6.9 %collective-permute-done.1.refs_1_ = bf16[2,528,128]{2,1,0:T(8,128)(2,1)S(1)} collective-permute-done((bf16[2,528,128]{2,1,0:T(8,128)(2,1)S(1)}, bf16[2,528,128]{2,1,0:T(8,128)(2,1)S(1)}, u32[]{:S(2)}, u32[]{:S(2)}) %collective-permute-start.1) | collective-permute-done | bytes 270368 | tf_op jit(solution)/shard_map/ppermute | solution.py:305
  89.6 6.3 %attend.5 = bf16[4,528,256]{2,1,0:T(8,128)(2,1)S(1)} custom-call(s32[8]{0:T(128)S(1)} %dynamic-slice_bitcast_fusion.info, bf16[4,272,512]{2,1,0:T(8,128)(2,1)S(1)} %bitcast.16, bf16[2,528,128]{2,1,0:T(8,128)(2,1)S(1)} %collective-permute-done.refs_0_, bf16[2,528,128]{2,1,0:T(8,128)(2,1)S(1)} %collective-permute-done.1.refs_1_, ...), custom_call_target="tpu_custom_call" | custom-call | flops 2684354560 | bytes 6291456 | tf_op jit(solution)/shard_map/attend/pallas_call | solution.py:190
  95.9 16.7 %all_to_all.10.parts = bf16[4,528,256]{2,1,0:T(8,128)(2,1)S(1)} all-to-all(bf16[4,528,256]{2,1,0:T(8,128)(2,1)S(1)} %attend.5), channel_id=1, replica_groups=mesh['y'=4,'z'=16,'x'=4,'core'=2] {'y'}, dimensions={0} | all-to-all | bytes 2162688 | tf_op jit(solution)/shard_map/all_to_all | solution.py:312
  112.6 0.3 combine.1
  112.9 3.9 %all-gather.2 = bf16[512,512]{1,0:T(8,128)(2,1)S(1)} all-gather(bf16[256,512]{1,0:T(8,128)(2,1)S(1)} %combine.1), channel_id=4, replica_groups=mesh['y'=4,'z'=16,'x'=4,'core'=2] {'core'}, dimensions={0}, use_global_device_ids=true | all-gather | bytes 786432 | tf_op jit(solution)/shard_map/all_gather | solution.py:313
  116.8 2.0 %project.1 = bf16[4,256,512]{2,1,0:T(8,128)(2,1)S(1)} custom-call(s32[1]{0:T(128)} %bitcast.core, bf16[2,256,512]{2,1,0:T(8,128)(2,1)S(1)} %bitcast.13, bf16[512,4096]{1,0:T(8,128)(2,1)S(1)} %copy-done, bf16[4,512,512]{2,1,0:T(8,128)(2,1)S(1)} %collective-permute-done.4.other_weight), custom_call_target="tpu_custom_call" | custom-call | tf_op jit(solution)/shard_map/project/pallas_call | solution.py:267
  118.8 18.1 %all_to_all.11 = bf16[4,256,512]{2,1,0:T(8,128)(2,1)S(1)} all-to-all(bf16[4,256,512]{2,1,0:T(8,128)(2,1)S(1)} %project.1), channel_id=1, replica_groups=mesh['y'=4,'z'=16,'x'=4,'core'=2] {'x'}, dimensions={0} | all-to-all | bytes 2097152 | tf_op jit(solution)/shard_map/all_to_all | solution.py:315
  136.9 0.9 reduce_sum.12
  (12 shorter events, 0.1 us)
Async XLA Ops:
  6.5 49.6 %all-gather.5.cloned.1.call-start = ((), (), s32[]{:S(2)}) async-start(), calls=%async_computation.2 | async-start | bytes 1392640 | tf_op jit(solution)/shard_map/all_gather | solution.py:298
  48.2 24.8 %collective-permute-start.2 = (bf16[4,528,128]{2,1,0:T(8,128)(2,1)S(1)}, bf16[4,528,128]{2,1,0:T(8,128)(2,1)S(1)}, u32[]{:S(2)}, u32[]{:S(2)}) collective-permute-start(bf16[4,528,128]{2,1,0:T(8,128)(2,1)S(1)} %bitcast.10), channel_id=1, source_target_pairs={{8,0},{16,8},{24,16},{160,24},{168,160},{176,168},{184,176},{320,1... | collective-permute-start | bytes 1622024 | tf_op jit(solution)/shard_map/ppermute | solution.py:302
  53.5 19.6 %collective-permute-start.3 = (bf16[4,528,128]{2,1,0:T(8,128)(2,1)S(1)}, bf16[4,528,128]{2,1,0:T(8,128)(2,1)S(1)}, u32[]{:S(2)}, u32[]{:S(2)}) collective-permute-start(bf16[4,528,128]{2,1,0:T(8,128)(2,1)S(1)} %bitcast.11), channel_id=1, source_target_pairs={{504,0},{0,8},{8,16},{16,24},{24,160},{160,168},{168,176},{176,184... | collective-permute-start | bytes 1622024 | tf_op jit(solution)/shard_map/ppermute | solution.py:303
  56.1 1.2 copy-start.1
  57.4 5.5 %copy-start = (bf16[512,4096]{1,0:T(8,128)(2,1)S(1)}, bf16[512,4096]{1,0:T(8,128)(2,1)}, u32[]{:S(2)}) copy-start(bf16[512,4096]{1,0:T(8,128)(2,1)} %own_weight.1) | copy-start | bytes 12582916
  63.3 53.5 %collective-permute-start.4 = (bf16[4,512,512]{2,1,0:T(8,128)(2,1)S(1)}, bf16[4,512,512]{2,1,0:T(8,128)(2,1)S(1)}, u32[]{:S(2)}, u32[]{:S(2)}) collective-permute-start(bf16[4,512,512]{2,1,0:T(8,128)(2,1)S(1)} %pack.1), channel_id=1, source_target_pairs={{0,1},{1,0},{2,3},{3,2},{4,5},{5,4},{6,7},{7,6},{8,9},{9,8},{10,11... | collective-permute-start | bytes 6291464 | tf_op jit(solution)/shard_map/ppermute | solution.py:309
  66.9 15.8 %collective-permute-start = (bf16[2,528,128]{2,1,0:T(8,128)(2,1)S(1)}, bf16[2,528,128]{2,1,0:T(8,128)(2,1)S(1)}, u32[]{:S(2)}, u32[]{:S(2)}) collective-permute-start(bf16[2,528,128]{2,1,0:T(8,128)(2,1)S(1)} %bitcast.18), channel_id=1, source_target_pairs={{16,0},{24,8},{160,16},{168,24},{176,160},{184,168},{320,176},{328... | collective-permute-start | bytes 811016 | tf_op jit(solution)/shard_map/ppermute | solution.py:304
  69.8 19.7 %collective-permute-start.1 = (bf16[2,528,128]{2,1,0:T(8,128)(2,1)S(1)}, bf16[2,528,128]{2,1,0:T(8,128)(2,1)S(1)}, u32[]{:S(2)}, u32[]{:S(2)}) collective-permute-start(bf16[2,528,128]{2,1,0:T(8,128)(2,1)S(1)} %bitcast.17), channel_id=1, source_target_pairs={{496,0},{504,8},{0,16},{8,24},{16,160},{24,168},{160,176},{168,184... | collective-permute-start | bytes 811016 | tf_op jit(solution)/shard_map/ppermute | solution.py:305
Sparse Core Ops, SparseCore 0:
  9.5 37.7 all-gather.4

commit v3 on v2

--- a/solution.py
+++ b/solution.py
@@ -40,18 +40,11 @@
     ]
 
 
-def run_on():
-    table = np.zeros((NY * NZ, 8), np.int32)
-    for y in range(NY - 1):
-        table[y * NZ + NZ - 1, 0:3] = 1, y, y + 1
-    return table
-
-
 def dot(a, b, dims):
     return lax.dot_general(a, b, (dims, ((), ())), preferred_element_type=F32)
 
 
-def attend_kernel(kinds, first, last, info, q_ref, *refs):
+def attend_kernel(kinds, first, last, y_ref, z_ref, q_ref, *refs):
     n_blocks = 1 + max(operand for kind in kinds for operand, _ in kind)
     blocks, refs = refs[:n_blocks], refs[n_blocks:]
     if first:
@@ -141,9 +134,9 @@
     lax.fori_loop(0, GROUP, head, 0)
 
     if kinds == AHEAD_BEHIND:
-        @pl.when(info[0] == 1)
+        @pl.when((z_ref[0] == NZ - 1) & (y_ref[0] < NY - 1))
         def _():
-            q, i = info[1], info[2]
+            q, i = y_ref[0], y_ref[0] + 1
             block = blocks[0].at[i]
             seen = jnp.concatenate([ids[0, i], ids[0, i]], axis=1) <= query_ids(q)
             for h in range(GROUP):
@@ -175,12 +168,11 @@
             ).astype(BF16)
 
 
-OWN = (((0, 0), (0, 1), (0, 2), (0, 3)),)
+OWN = FAR = (((0, 0), (0, 1), (0, 2), (0, 3)),)
 AHEAD_BEHIND = (((0, 0), (0, 1), (0, 2), (0, 3)), ((1, 0), (1, 1), (1, 2), (1, 3)))
-FAR = (((0, 0), (0, 1), (1, 0), (1, 1)),)
-
-
-def attend(kinds, first, last, info, q, blocks, state):
+
+
+def attend(kinds, first, last, place, q, blocks, state):
     vmem = pl.BlockSpec(memory_space=pltpu.VMEM)
     n = len(kinds)
     acc = jax.ShapeDtypeStruct((4, GROUP, VROWS, TOK), F32)
@@ -190,7 +182,8 @@
     return pl.pallas_call(
         functools.partial(attend_kernel, kinds, first, last),
         out_shape=jax.ShapeDtypeStruct((4, OROWS, TOK), BF16) if last else (acc, row_max),
-        in_specs=[pl.BlockSpec(memory_space=pltpu.SMEM)] + [vmem] * (1 + len(blocks) + len(state)),
+        in_specs=[pl.BlockSpec(memory_space=pltpu.SMEM)] * 2
+        + [vmem] * (1 + len(blocks) + len(state)),
         out_specs=vmem if last else (vmem, vmem),
         scratch_shapes=(running if last else [])
         + [
@@ -205,7 +198,7 @@
             flops=scores * 8 * HEAD, transcendentals=scores, bytes_accessed=6 * 2**20
         ),
         name="attend",
-    )(info, q, *blocks, *state)
+    )(*place, q, *blocks, *state)
 
 
 def combine_kernel(parts, out_ref):
@@ -282,33 +275,57 @@
     )(core, both, own_weight, other_weight)
 
 
-def split_ids(block_ids):
-    return (block_ids // 32).astype(BF16), (block_ids % 32).astype(BF16)
+def stage_kernel(q, k, v, ids, q_out, block_out):
+    high = (ids[...] >> 5).astype(F32)
+    low = (ids[...] & 31).astype(F32)
+    q_out[0:TOK, :] = q[...]
+    terms = (high[0:1], high[1:2], low[0:1], low[1:2])
+    for n, term in enumerate(terms):
+        q_out[TOK:QROWS, n * 128 : (n + 1) * 128] = jnp.broadcast_to(term, (16, 128)).astype(BF16)
+    block_out[0:TOK, :] = k[...]
+    block_out[TOK : 2 * TOK, :] = v[...]
+    block_out[2 * TOK : ROWS, :] = jnp.concatenate(
+        [high, low, jnp.zeros((12, 128), F32)], axis=0
+    ).astype(BF16)
+
+
+def stage(q, k, v, ids):
+    vmem = pl.BlockSpec(memory_space=pltpu.VMEM)
+    return pl.pallas_call(
+        stage_kernel,
+        out_shape=(
+            jax.ShapeDtypeStruct((QROWS, WIDTH), BF16),
+            jax.ShapeDtypeStruct((ROWS, HEAD), BF16),
+        ),
+        in_specs=[vmem] * 4,
+        out_specs=(vmem, vmem),
+        compiler_params=pltpu.CompilerParams(vmem_limit_bytes=56 * 2**20),
+        name="stage",
+    )(q, k, v, ids)
 
 
 def local(queries, keys, values, block_ids, out_weight):
     ctx = ("y", "z")
-    high, low = split_ids(block_ids)
-    info = lax.dynamic_index_in_dim(
-        jnp.asarray(run_on()), lax.axis_index(ctx), 0, keepdims=False
-    )
+    place = [lax.axis_index(axis).reshape(1) for axis in ctx]
     core = lax.axis_index("core").reshape(1)
 
-    q_ids = jnp.zeros((16, GROUP * HEAD), BF16).at[0].set(jnp.concatenate([high, low]))
-    q_all = lax.all_gather(jnp.concatenate([queries, q_ids], axis=0), "y", axis=0)
-    id_rows = jnp.concatenate([high, low]).reshape(4, 128)
-    block = jnp.concatenate([keys, values, id_rows, jnp.zeros((12, 128), BF16)], axis=0)
+    staged, block = stage(queries, keys, values, block_ids.reshape(2, 128))
+    q_all = lax.all_gather(staged, "y", axis=0)
     own = lax.all_gather(block, ctx, axis=0, axis_index_groups=ring_groups())
     ahead = lax.ppermute(own, ctx, ring_step(1))
     behind = lax.ppermute(own, ctx, ring_step(-1))
-    far_low = lax.ppermute(own[0:2], ctx, ring_step(2))
-    far_high = lax.ppermute(own[2:4], ctx, ring_step(-2))
-
-    state = attend(OWN, True, False, info, q_all, [own], ())
-    weight, state = lax.optimization_barrier((out_weight, state))
+
+    state = attend(OWN, True, False, place, q_all, [own], ())
+    sent, state = lax.optimization_barrier((own, state))
+    far = lax.ppermute(
+        sent,
+        (*ctx, "core"),
+        [(2 * a + c, 2 * b + c) for c in range(2) for a, b in ring_step(2 - 4 * c)],
+    )
+    state = attend(AHEAD_BEHIND, False, False, place, q_all, [ahead, behind], state)
+    partial = attend(FAR, False, True, place, q_all, [far], state)
+    weight, partial = lax.optimization_barrier((out_weight, partial))
     other_weight = lax.ppermute(pack(core, weight), "core", [(0, 1), (1, 0)])
-    state = attend(AHEAD_BEHIND, False, False, info, q_all, [ahead, behind], state)
-    partial = attend(FAR, False, True, info, q_all, [far_low, far_high], state)
     partial = lax.all_to_all(partial, "y", 0, 0, tiled=True)
     both = lax.all_gather(combine(partial), "core", axis=0)
     share = project(core, both, out_weight, other_weight)

time: 145 us -> 139 us (0.959)
  starting transfers between devices: 16.9 us -> 12.6 us
  other arithmetic: 3.3 us -> 0.9 us
  waiting for transfers between devices: 6.92 us -> 4.96 us
  blocking collectives: 76 us -> 77.8 us
    ppermute x2 -> x1, starting transfers between devices: 6.18 us -> 1.91 us  [local(): lax.ppermute(sent, (*ctx, 'core'), [(2 * a + c, 2 * b + c) for c in range...]
    unnamed x4 -> x10, local copies, waits for them, and re-layouts: 1.25 us -> 4.32 us
    all_to_all x1, blocking collectives: 16.7 us -> 18.9 us  [local(): partial = lax.all_to_all(partial, 'y', 0, 0, tiled=True)]
    ppermute x2 -> x1, waiting for transfers between devices: 6.9 us -> 4.91 us  [local(): lax.ppermute(sent, (*ctx, 'core'), [(2 * a + c, 2 * b + c) for c in range...]
    concatenate x1 -> x0, local copies, waits for them, and re-layouts: 1.84 us -> none  [local(): jnp.concatenate([keys, values, id_rows, jnp.zeros((12, 128), BF16)], axis=0)]
    pallas_call x0 -> x1, Pallas kernels: none -> 1.77 us  [stage(): pl.pallas_call(stage_kernel, out_shape=(jax.ShapeDtypeStruct((QROWS, WIDT...]
    concatenate x2 -> x0, other arithmetic: 1.71 us -> none  [the longest x1 1.7 us: local(): jnp.concatenate([queries, q_ids], axis=0)]
    pallas_call x3, Pallas kernels: 21.4 us -> 19.7 us  [attend(): pl.pallas_call(functools.partial(attend_kernel, kinds, first, last), out_...]
  transfers between devices with their start and end apart: 6 -> 5, of which waited for: 1 -> 1; matrix products, arithmetic and copies ran while one was open for 2% -> 0% of each run, Pallas kernels for 15% -> 10%
where the time goes in v3:
time: 139 us; the launch traced here: 138 us
  blocking collectives  77.8 us (56%)
  Pallas kernels  24.2 us (17%)
  between operations  13.5 us (10%)
  starting transfers between devices  12.6 us (9%)
  waiting for transfers between devices  4.96 us (4%)
  local copies, waits for them, and re-layouts  4.32 us (3%)
    all_gather x1, blocking collectives, local(): own = lax.all_gather(block, ctx, axis=0, axis_index_groups=ring_groups())  37.6 us
    pallas_call x3, Pallas kernels, attend(): pl.pallas_call(functools.partial(attend_kernel, kinds, first, last), out_...  19.7 us
    all_to_all x1, blocking collectives, local(): partial = lax.all_to_all(partial, 'y', 0, 0, tiled=True)  18.9 us
    all_to_all x1, blocking collectives, local(): shares = lax.all_to_all(share, 'x', 0, 0, tiled=True)  18 us
    ppermute x1, starting transfers between devices, local(): ahead = lax.ppermute(own, ctx, ring_step(1))  6.08 us
    ppermute x1, waiting for transfers between devices, local(): lax.ppermute(sent, (*ctx, 'core'), [(2 * a + c, 2 * b + c) for c in range...  4.91 us
    unnamed x10, local copies, waits for them, and re-layouts  4.32 us
    all_gather x1, blocking collectives, local(): both = lax.all_gather(combine(partial), 'core', axis=0)  3.22 us
  transfers between devices with their start and end apart: 5, of which 1 were waited for; matrix products, arithmetic and copies ran while one was open for 0% of the time, Pallas kernels for 10%

profile of v3, /device:TPU:1, one launch (start us, length us, event | category | flops | bytes accessed | tf_op | source)
XLA Modules:
  0.0 138.3 jit_solution(9600030523053340991)
XLA Ops:
  6.5 1.8 %stage.1 = (bf16[272,512]{1,0:T(8,128)(2,1)}, bf16[528,128]{1,0:T(8,128)(2,1)}) custom-call(bf16[256,512]{1,0:T(8,128)(2,1)} %q.1, bf16[256,128]{1,0:T(8,128)(2,1)} %k.1, bf16[256,128]{1,0:T(8,128)(2,1)} %v.1, s32[2,128]{1,0:T(2,128)} %bitcast.15), custom_call_target="tpu_custom_call" | custom-call | tf_op jit(solution)/shard_map/stage/pallas_call | solution.py:294
  8.3 0.0 all-gather.5.cloned.1.call-update
  8.3 37.6 %all-gather.1 = bf16[2112,128]{1,0:T(8,128)(2,1)S(1)} all-gather(bf16[528,128]{1,0:T(8,128)(2,1)} %get-tuple-element.17), channel_id=3, replica_groups={{0,160,320,480},{8,168,328,488},{16,176,336,496},{24,184,344,504},{32,1..., dimensions={0}, use_global_device_ids=true | all-gather | bytes 675840 | tf_op jit(solution)/shard_map/all_gather | solution.py:314
  45.9 2.5 %collective-permute-start.2 = (bf16[4,528,128]{2,1,0:T(8,128)(2,1)S(1)}, bf16[4,528,128]{2,1,0:T(8,128)(2,1)S(1)}, u32[]{:S(2)}, u32[]{:S(2)}) collective-permute-start(bf16[4,528,128]{2,1,0:T(8,128)(2,1)S(1)} %bitcast.8), channel_id=1, source_target_pairs={{504,0},{0,8},{8,16},{16,24},{24,160},{160,168},{168,176},{176,184... | collective-permute-start | bytes 1622024 | tf_op jit(solution)/shard_map/ppermute | solution.py:316
  48.4 6.1 %collective-permute-start.1 = (bf16[4,528,128]{2,1,0:T(8,128)(2,1)S(1)}, bf16[4,528,128]{2,1,0:T(8,128)(2,1)S(1)}, u32[]{:S(2)}, u32[]{:S(2)}) collective-permute-start(bf16[4,528,128]{2,1,0:T(8,128)(2,1)S(1)} %bitcast.9), channel_id=1, source_target_pairs={{8,0},{16,8},{24,16},{160,24},{168,160},{176,168},{184,176},{320,1... | collective-permute-start | bytes 1622024 | tf_op jit(solution)/shard_map/ppermute | solution.py:315
  54.5 0.0 all-gather.5.cloned.1.call-done
  54.6 1.2 copy-done.1
  55.8 4.9 %attend.3 = (f32[4,4,144,256]{3,2,1,0:T(8,128)S(1)}, f32[4,4,1,256]{3,2,1,0:T(1,128)S(1)}) custom-call(s32[1]{0:T(128)} %bitcast.1.y_ref, s32[1]{0:T(128)} %bitcast.2.z_ref, bf16[4,272,512]{2,1,0:T(8,128)(2,1)S(1)} %bitcast.12, bf16[4,528,128]{2,1,0:T(8,128)(2,1)S(1)} %bitcast.10), custom_call_target="tpu_custom_call" | custom-call | flops 2684354560 | bytes 6291456 | tf_op jit(solution)/shard_map/attend/pallas_call | solution.py:182
  60.7 1.4 %copy-done.3 = f32[4,4,144,256]{3,2,1,0:T(8,128)} copy-done((f32[4,4,144,256]{3,2,1,0:T(8,128)}, f32[4,4,144,256]{3,2,1,0:T(8,128)S(1)}, u32[]{:S(2)}) %copy-start.3) | copy-done | bytes 2359320
  62.2 1.9 %collective-permute-start = (bf16[4,528,128]{2,1,0:T(8,128)(2,1)S(1)}, bf16[4,528,128]{2,1,0:T(8,128)(2,1)S(1)}, u32[]{:S(2)}, u32[]{:S(2)}) collective-permute-start(bf16[4,528,128]{2,1,0:T(8,128)(2,1)S(1)} %bitcast.11), channel_id=1, source_target_pairs={{16,0},{24,8},{160,16},{168,24},{176,160},{184,168},{320,176},{328... | collective-permute-start | bytes 1622024 | tf_op jit(solution)/shard_map/ppermute | solution.py:320
  64.1 0.0 collective-permute-done.2.refs_1_
  64.1 0.0 collective-permute-done.1.refs_0_
  64.1 1.7 %copy-done.4 = f32[4,4,144,256]{3,2,1,0:T(8,128)S(1)} copy-done((f32[4,4,144,256]{3,2,1,0:T(8,128)S(1)}, f32[4,4,144,256]{3,2,1,0:T(8,128)}, u32[]{:S(2)}) %copy-start.4) | copy-done | bytes 2359320
  65.8 9.0 %attend.4 = (f32[4,4,144,256]{3,2,1,0:T(8,128)S(1)}, f32[4,4,1,256]{3,2,1,0:T(1,128)S(1)}) custom-call(s32[1]{0:T(128)} %bitcast.1.y_ref, s32[1]{0:T(128)} %bitcast.2.z_ref, bf16[4,272,512]{2,1,0:T(8,128)(2,1)S(1)} %bitcast.13, bf16[4,528,128]{2,1,0:T(8,128)(2,1)S(1)} %collective-permute-done.1.refs_0_, ...), custom_call_target="tpu_custom_call" | custom-call | flops 5368709120 | bytes 6291456 | tf_op jit(solution)/shard_map/attend/pallas_call | solution.py:182
  74.8 4.9 %collective-permute-done.refs_0_ = bf16[4,528,128]{2,1,0:T(8,128)(2,1)S(1)} collective-permute-done((bf16[4,528,128]{2,1,0:T(8,128)(2,1)S(1)}, bf16[4,528,128]{2,1,0:T(8,128)(2,1)S(1)}, u32[]{:S(2)}, u32[]{:S(2)}) %collective-permute-start) | collective-permute-done | bytes 540704 | tf_op jit(solution)/shard_map/ppermute | solution.py:320
  79.7 5.8 %attend.5 = bf16[4,528,256]{2,1,0:T(8,128)(2,1)S(1)} custom-call(s32[1]{0:T(128)} %bitcast.1.y_ref, s32[1]{0:T(128)} %bitcast.2.z_ref, bf16[4,272,512]{2,1,0:T(8,128)(2,1)S(1)} %bitcast.14, bf16[4,528,128]{2,1,0:T(8,128)(2,1)S(1)} %collective-permute-done.refs_0_, f32[4,4,144,256]{3,2,1,0:T(8,128)S(1)} %get-tuple-element.23.refs_1_, ...), custom_call_target="tpu_custom_call" | custom-call | flops 2684354560 | bytes 6291456 | tf_op jit(solution)/shard_map/attend/pallas_call | solution.py:182
  85.5 0.4 pack.1
  85.9 2.1 %collective-permute-start.3 = (bf16[4,512,512]{2,1,0:T(8,128)(2,1)S(1)}, bf16[4,512,512]{2,1,0:T(8,128)(2,1)S(1)}, u32[]{:S(2)}, u32[]{:S(2)}) collective-permute-start(bf16[4,512,512]{2,1,0:T(8,128)(2,1)S(1)} %pack.1), channel_id=1, source_target_pairs={{0,1},{1,0},{2,3},{3,2},{4,5},{5,4},{6,7},{7,6},{8,9},{9,8},{10,11... | collective-permute-start | bytes 6291464 | tf_op jit(solution)/shard_map/ppermute | solution.py:328
  88.1 18.9 %all_to_all.10.parts = bf16[4,528,256]{2,1,0:T(8,128)(2,1)S(1)} all-to-all(bf16[4,528,256]{2,1,0:T(8,128)(2,1)S(1)} %attend.5), channel_id=1, replica_groups=mesh['y'=4,'z'=16,'x'=4,'core'=2] {'y'}, dimensions={0} | all-to-all | bytes 2162688 | tf_op jit(solution)/shard_map/all_to_all | solution.py:329
  107.0 0.3 combine.1
  107.3 3.2 %all-gather.2 = bf16[512,512]{1,0:T(8,128)(2,1)S(1)} all-gather(bf16[256,512]{1,0:T(8,128)(2,1)S(1)} %combine.1), channel_id=4, replica_groups=mesh['y'=4,'z'=16,'x'=4,'core'=2] {'core'}, dimensions={0}, use_global_device_ids=true | all-gather | bytes 786432 | tf_op jit(solution)/shard_map/all_gather | solution.py:330
  110.5 2.0 %project.1 = bf16[4,256,512]{2,1,0:T(8,128)(2,1)S(1)} custom-call(s32[1]{0:T(128)} %bitcast.core, bf16[2,256,512]{2,1,0:T(8,128)(2,1)S(1)} %bitcast.7, bf16[512,4096]{1,0:T(8,128)(2,1)S(1)} %copy-done, bf16[4,512,512]{2,1,0:T(8,128)(2,1)S(1)} %collective-permute-done.3.other_weight), custom_call_target="tpu_custom_call" | custom-call | tf_op jit(solution)/shard_map/project/pallas_call | solution.py:260
  112.5 18.0 %all_to_all.11 = bf16[4,256,512]{2,1,0:T(8,128)(2,1)S(1)} all-to-all(bf16[4,256,512]{2,1,0:T(8,128)(2,1)S(1)} %project.1), channel_id=1, replica_groups=mesh['y'=4,'z'=16,'x'=4,'core'=2] {'x'}, dimensions={0} | all-to-all | bytes 2097152 | tf_op jit(solution)/shard_map/all_to_all | solution.py:332
  130.5 0.9 reduce_sum.12
  (9 shorter events, 0.0 us)
Async XLA Ops:
  6.5 48.0 %all-gather.5.cloned.1.call-start = ((), (), s32[]{:S(2)}) async-start(), calls=%async_computation.2 | async-start | bytes 1392640 | tf_op jit(solution)/shard_map/all_gather | solution.py:313
  45.9 18.2 %collective-permute-start.2 = (bf16[4,528,128]{2,1,0:T(8,128)(2,1)S(1)}, bf16[4,528,128]{2,1,0:T(8,128)(2,1)S(1)}, u32[]{:S(2)}, u32[]{:S(2)}) collective-permute-start(bf16[4,528,128]{2,1,0:T(8,128)(2,1)S(1)} %bitcast.8), channel_id=1, source_target_pairs={{504,0},{0,8},{8,16},{16,24},{24,160},{160,168},{168,176},{176,184... | collective-permute-start | bytes 1622024 | tf_op jit(solution)/shard_map/ppermute | solution.py:316
  48.4 15.7 %collective-permute-start.1 = (bf16[4,528,128]{2,1,0:T(8,128)(2,1)S(1)}, bf16[4,528,128]{2,1,0:T(8,128)(2,1)S(1)}, u32[]{:S(2)}, u32[]{:S(2)}) collective-permute-start(bf16[4,528,128]{2,1,0:T(8,128)(2,1)S(1)} %bitcast.9), channel_id=1, source_target_pairs={{8,0},{16,8},{24,16},{160,24},{168,160},{176,168},{184,176},{320,1... | collective-permute-start | bytes 1622024 | tf_op jit(solution)/shard_map/ppermute | solution.py:315
  54.6 1.2 copy-start.1
  55.8 8.3 %copy-start.2 = (bf16[1088,512]{1,0:T(8,128)(2,1)S(1)}, bf16[1088,512]{1,0:T(8,128)(2,1)}, u32[]{:S(2)}) copy-start(bf16[1088,512]{1,0:T(8,128)(2,1)} %all-gather.5.cloned.1.call-done) | copy-start | bytes 3342340
  60.7 1.4 %copy-start.3 = (f32[4,4,144,256]{3,2,1,0:T(8,128)}, f32[4,4,144,256]{3,2,1,0:T(8,128)S(1)}, u32[]{:S(2)}) copy-start(f32[4,4,144,256]{3,2,1,0:T(8,128)S(1)} %get-tuple-element.21.refs_2_) | copy-start | bytes 7077892
  62.2 17.6 %collective-permute-start = (bf16[4,528,128]{2,1,0:T(8,128)(2,1)S(1)}, bf16[4,528,128]{2,1,0:T(8,128)(2,1)S(1)}, u32[]{:S(2)}, u32[]{:S(2)}) collective-permute-start(bf16[4,528,128]{2,1,0:T(8,128)(2,1)S(1)} %bitcast.11), channel_id=1, source_target_pairs={{16,0},{24,8},{160,16},{168,24},{176,160},{184,168},{320,176},{328... | collective-permute-start | bytes 1622024 | tf_op jit(solution)/shard_map/ppermute | solution.py:320
  64.1 1.7 %copy-start.4 = (f32[4,4,144,256]{3,2,1,0:T(8,128)S(1)}, f32[4,4,144,256]{3,2,1,0:T(8,128)}, u32[]{:S(2)}) copy-start(f32[4,4,144,256]{3,2,1,0:T(8,128)} %copy-done.3) | copy-start | bytes 7077892
  79.7 5.8 %copy-start = (bf16[512,4096]{1,0:T(8,128)(2,1)S(1)}, bf16[512,4096]{1,0:T(8,128)(2,1)}, u32[]{:S(2)}) copy-start(bf16[512,4096]{1,0:T(8,128)(2,1)} %own_weight.1) | copy-start | bytes 12582916
  85.9 24.6 %collective-permute-start.3 = (bf16[4,512,512]{2,1,0:T(8,128)(2,1)S(1)}, bf16[4,512,512]{2,1,0:T(8,128)(2,1)S(1)}, u32[]{:S(2)}, u32[]{:S(2)}) collective-permute-start(bf16[4,512,512]{2,1,0:T(8,128)(2,1)S(1)} %pack.1), channel_id=1, source_target_pairs={{0,1},{1,0},{2,3},{3,2},{4,5},{5,4},{6,7},{7,6},{8,9},{9,8},{10,11... | collective-permute-start | bytes 6291464 | tf_op jit(solution)/shard_map/ppermute | solution.py:328
Sparse Core Ops, SparseCore 0:
  9.5 38.0 all-gather.4

commit v4 on v3

--- a/solution.py
+++ b/solution.py
@@ -44,9 +44,9 @@
     return lax.dot_general(a, b, (dims, ((), ())), preferred_element_type=F32)
 
 
-def attend_kernel(kinds, first, last, y_ref, z_ref, q_ref, *refs):
-    n_blocks = 1 + max(operand for kind in kinds for operand, _ in kind)
-    blocks, refs = refs[:n_blocks], refs[n_blocks:]
+def attend_kernel(steps, first, last, y_ref, z_ref, q_ref, *refs):
+    kinds = len(steps)
+    blocks, refs = refs[:kinds], refs[kinds:]
     if first:
         acc_in = max_in = None
     else:
@@ -55,56 +55,41 @@
         out_ref, acc, row_max, *refs = refs
     else:
         acc, row_max, *refs = refs
-    v_buf, even, odd, top, ids = refs
-    scores = (even, odd)
+    v_buf, score_1, score_2, score_3, top = refs
+    scores = (None, score_1, score_2, score_3)
 
     def key_block(n, i):
-        operand, index = kinds[n][i]
-        return blocks[operand].at[index]
-
-    for n in range(len(kinds)):
+        return blocks[n].at[i]
+
+    for n in range(kinds):
         for i in range(4):
-            block = key_block(n, i)
-            v_buf[n, i, 0:HEAD, :] = block[TOK : 2 * TOK, :].T
+            v_buf[n, i, 0:HEAD, :] = key_block(n, i)[TOK : 2 * TOK, :].T
             v_buf[n, i, HEAD:VROWS, :] = jnp.ones((16, TOK), BF16)
-            rows = block[2 * TOK : 2 * TOK + 16, :].astype(F32)
-            for half in range(2):
-                line = rows[half : half + 1, :] * 32.0 + rows[half + 2 : half + 3, :]
-                ids[n, i, half * 128 : half * 128 + 128, :] = jnp.broadcast_to(line, (128, 128)).T
 
     def query(q, h):
         return q_ref[q, 0:TOK, pl.ds(pl.multiple_of(h * HEAD, HEAD), HEAD)]
 
-    def query_ids(q):
-        tail = q_ref[q, TOK : TOK + 16, :].astype(F32)
-        return (tail[:, 0:TOK] * 32.0 + tail[:, TOK : 2 * TOK])[0:1, :]
-
-    def hide(s, q, n, i):
-        seen = jnp.concatenate([ids[n, i], ids[n, i]], axis=1) <= query_ids(q)
-        return jnp.where(seen, s, HIDDEN)
-
     def score(q, h, n, i):
-        s = dot(key_block(n, i)[0:TOK, :], query(q, h), ((1,), (1,)))
-        return hide(s, q, n, i) if i == q else s
+        return dot(key_block(n, i)[0:TOK, :], query(q, h), ((1,), (1,)))
 
     def fold(s):
         return jnp.max(s.reshape(TOK // 8, 8, TOK), axis=0)
 
-    parts = [[(n, i) for i in range(q + 1) for n in range(len(kinds))] for q in range(4)]
+    parts = [[(n, i) for i in range(q) for n in range(kinds)] for q in range(4)]
 
     def score_into(q, h, at, best):
         s = score(q, h, *parts[q][at])
-        scores[q % 2][at * TOK : (at + 1) * TOK, :] = s
+        scores[q][at * TOK : (at + 1) * TOK, :] = s
         return fold(s) if best is None else jnp.maximum(best, fold(s))
 
     best = None
-    for at in range(len(parts[0])):
-        best = score_into(0, 0, at, best)
+    for at in range(len(parts[1])):
+        best = score_into(1, 0, at, best)
     top[...] = best
 
     def head(h, carry):
-        for q in range(4):
-            q_next, h_next = (q + 1, h) if q < 3 else (0, jnp.minimum(h + 1, GROUP - 1))
+        for q in range(1, 4):
+            q_next, h_next = (q + 1, h) if q < 3 else (1, jnp.minimum(h + 1, GROUP - 1))
             peak = jnp.max(top[...], axis=0, keepdims=True)
             if first:
                 new = jnp.maximum(peak, FLOOR)
@@ -123,7 +108,7 @@
                     best = score_into(q_next, h_next, other, best)
                 done = until
                 weights = jnp.exp2(
-                    (scores[q % 2][at * TOK : (at + 1) * TOK, :] - new) * LOG_SCALE
+                    (scores[q][at * TOK : (at + 1) * TOK, :] - new) * LOG_SCALE
                 ).astype(BF16)
                 part = dot(v_buf[n, i], weights, ((1,), (0,)))
                 total = part if total is None else total + part
@@ -133,22 +118,52 @@
 
     lax.fori_loop(0, GROUP, head, 0)
 
-    if kinds == AHEAD_BEHIND:
-        @pl.when((z_ref[0] == NZ - 1) & (y_ref[0] < NY - 1))
-        def _():
-            q, i = y_ref[0], y_ref[0] + 1
-            block = blocks[0].at[i]
-            seen = jnp.concatenate([ids[0, i], ids[0, i]], axis=1) <= query_ids(q)
-            for h in range(GROUP):
-                s = dot(block[0:TOK, :], query(q, h), ((1,), (1,)))
-                s = jnp.where(seen, s, HIDDEN)
-                old = row_max[q, h]
-                new = jnp.maximum(old, jnp.max(s, axis=0, keepdims=True))
-                weights = jnp.exp2((s - new) * LOG_SCALE).astype(BF16)
-                acc[q, h] = acc[q, h] * jnp.exp2((old - new) * LOG_SCALE) + dot(
-                    v_buf[0, i], weights, ((1,), (0,))
-                )
-                row_max[q, h] = new
+    if first:
+        acc[0] = jnp.zeros((GROUP, VROWS, TOK), F32)
+        row_max[0] = jnp.full((GROUP, 1, TOK), FLOOR, F32)
+    else:
+        acc[0] = acc_in[0]
+        row_max[0] = max_in[0]
+
+    def by_number(n, q, i):
+        rows = key_block(n, i)[2 * TOK : 2 * TOK + 16, :].astype(F32)
+        key_ids = []
+        for half in range(2):
+            line = rows[half : half + 1, :] * 32.0 + rows[half + 2 : half + 3, :]
+            key_ids.append(jnp.broadcast_to(line, (128, 128)).T)
+        key_ids = jnp.concatenate(key_ids, axis=0)
+        tail = q_ref[q, TOK : TOK + 16, :].astype(F32)
+        query_ids = (tail[:, 0:TOK] * 32.0 + tail[:, TOK : 2 * TOK])[0:1, :]
+        seen = jnp.concatenate([key_ids, key_ids], axis=1) <= query_ids
+        s = score(q, 0, n, i)
+        for h in range(GROUP):
+            s_next = score(q, h + 1, n, i) if h + 1 < GROUP else None
+            s = jnp.where(seen, s, HIDDEN)
+            old = row_max[q, h]
+            new = jnp.maximum(old, jnp.max(s, axis=0, keepdims=True))
+            weights = jnp.exp2((s - new) * LOG_SCALE).astype(BF16)
+            acc[q, h] = acc[q, h] * jnp.exp2((old - new) * LOG_SCALE) + dot(
+                v_buf[n, i], weights, ((1,), (0,))
+            )
+            row_max[q, h] = new
+            s = s_next
+
+    y, z = y_ref[0], z_ref[0]
+    d = (z // 4 + 4 - y) % 4
+    for n, step in enumerate(steps):
+        kind = (z + step + 4) % 4
+        count = jnp.minimum((z + 5 - kind) // 4, 4)
+
+        def run(t, carry, n=n):
+            q = (t + 4 - d) % 4
+            by_number(n, q, q)
+            return carry
+
+        lax.fori_loop(0, count, run, 0)
+        if step == 1:
+            @pl.when((z == NZ - 1) & (y < NY - 1))
+            def _(n=n):
+                by_number(n, y, y + 1)
 
     if last:
         for q in range(4):
@@ -168,32 +183,29 @@
             ).astype(BF16)
 
 
-OWN = FAR = (((0, 0), (0, 1), (0, 2), (0, 3)),)
-AHEAD_BEHIND = (((0, 0), (0, 1), (0, 2), (0, 3)), ((1, 0), (1, 1), (1, 2), (1, 3)))
-
-
-def attend(kinds, first, last, place, q, blocks, state):
+def attend(steps, first, last, place, q, blocks, state):
     vmem = pl.BlockSpec(memory_space=pltpu.VMEM)
-    n = len(kinds)
+    n = len(steps)
     acc = jax.ShapeDtypeStruct((4, GROUP, VROWS, TOK), F32)
     row_max = jax.ShapeDtypeStruct((4, GROUP, 1, TOK), F32)
     running = [pltpu.VMEM(acc.shape, F32), pltpu.VMEM(row_max.shape, F32)]
     scores = 10 * n * 4 * TOK * TOK
     return pl.pallas_call(
-        functools.partial(attend_kernel, kinds, first, last),
+        functools.partial(attend_kernel, steps, first, last),
         out_shape=jax.ShapeDtypeStruct((4, OROWS, TOK), BF16) if last else (acc, row_max),
         in_specs=[pl.BlockSpec(memory_space=pltpu.SMEM)] * 2
         + [vmem] * (1 + len(blocks) + len(state)),
         out_specs=vmem if last else (vmem, vmem),
+        input_output_aliases={} if first or last else {3 + n: 0, 4 + n: 1},
         scratch_shapes=(running if last else [])
         + [
             pltpu.VMEM((n, 4, VROWS, TOK), BF16),
+            pltpu.VMEM((n * TOK, TOK), F32),
+            pltpu.VMEM((2 * n * TOK, TOK), F32),
             pltpu.VMEM((3 * n * TOK, TOK), F32),
-            pltpu.VMEM((4 * n * TOK, TOK), F32),
             pltpu.VMEM((8, TOK), F32),
-            pltpu.VMEM((n, 4, TOK, 128), F32),
         ],
-        compiler_params=pltpu.CompilerParams(vmem_limit_bytes=32 * 2**20),
+        compiler_params=pltpu.CompilerParams(vmem_limit_bytes=20 * 2**20),
         cost_estimate=pl.CostEstimate(
             flops=scores * 8 * HEAD, transcendentals=scores, bytes_accessed=6 * 2**20
         ),
@@ -315,17 +327,17 @@
     ahead = lax.ppermute(own, ctx, ring_step(1))
     behind = lax.ppermute(own, ctx, ring_step(-1))
 
-    state = attend(OWN, True, False, place, q_all, [own], ())
-    sent, state = lax.optimization_barrier((own, state))
+    state = attend((0,), True, False, place, q_all, [own], ())
+    weight, row_max = lax.optimization_barrier((out_weight, state[1]))
+    state = (state[0], row_max)
+    other_weight = lax.ppermute(pack(core, weight), "core", [(0, 1), (1, 0)])
     far = lax.ppermute(
-        sent,
+        jnp.where(core == 0, ahead, behind),
         (*ctx, "core"),
-        [(2 * a + c, 2 * b + c) for c in range(2) for a, b in ring_step(2 - 4 * c)],
+        [(2 * a + c, 2 * b + c) for c in range(2) for a, b in ring_step(1 - 2 * c)],
     )
-    state = attend(AHEAD_BEHIND, False, False, place, q_all, [ahead, behind], state)
-    partial = attend(FAR, False, True, place, q_all, [far], state)
-    weight, partial = lax.optimization_barrier((out_weight, partial))
-    other_weight = lax.ppermute(pack(core, weight), "core", [(0, 1), (1, 0)])
+    state = attend((1, -1), False, False, place, q_all, [ahead, behind], state)
+    partial = attend((2,), False, True, place, q_all, [far], state)
     partial = lax.all_to_all(partial, "y", 0, 0, tiled=True)
     both = lax.all_gather(combine(partial), "core", axis=0)
     share = project(core, both, out_weight, other_weight)

time: 139 us -> 136 us (0.978)
  waiting for transfers between devices: 4.96 us -> 10.8 us
  Pallas kernels: 24.2 us -> 19.8 us
  local copies, waits for them, and re-layouts: 4.32 us -> 1.24 us
  blocking collectives: 77.8 us -> 76.2 us
    ppermute x1, waiting for transfers between devices: 0.01 us -> 6.5 us  [local(): behind = lax.ppermute(own, ctx, ring_step(-1))]
    pallas_call x3, Pallas kernels: 19.7 us -> 15.4 us  [attend(): pl.pallas_call(functools.partial(attend_kernel, steps, first, last), out_...]
    unnamed x10 -> x4, local copies, waits for them, and re-layouts: 4.32 us -> 1.24 us
    ppermute x1, starting transfers between devices: 2.13 us -> 3.53 us  [local(): other_weight = lax.ppermute(pack(core, weight), 'core', [(0, 1), (1, 0)])]
  transfers between devices with their start and end apart: 5 -> 5, of which waited for: 1 -> 2; matrix products, arithmetic and copies ran while one was open for 0% -> 0% of each run, Pallas kernels for 10% -> 12%
where the time goes in v4:
time: 136 us; the launch traced here: 135 us
  blocking collectives  76.2 us (56%)
  Pallas kernels  19.8 us (15%)
  between operations  13.5 us (10%)
  starting transfers between devices  12.6 us (9%)
  waiting for transfers between devices  10.8 us (8%)
    all_gather x1, blocking collectives, local(): own = lax.all_gather(block, ctx, axis=0, axis_index_groups=ring_groups())  37.6 us
    all_to_all x1, blocking collectives, local(): shares = lax.all_to_all(share, 'x', 0, 0, tiled=True)  18 us
    all_to_all x1, blocking collectives, local(): partial = lax.all_to_all(partial, 'y', 0, 0, tiled=True)  17.6 us
    pallas_call x3, Pallas kernels, attend(): pl.pallas_call(functools.partial(attend_kernel, steps, first, last), out_...  15.4 us
    ppermute x1, waiting for transfers between devices, local(): behind = lax.ppermute(own, ctx, ring_step(-1))  6.5 us
    ppermute x1, starting transfers between devices, local(): ahead = lax.ppermute(own, ctx, ring_step(1))  5.28 us
    ppermute x1, waiting for transfers between devices, local(): lax.ppermute(jnp.where(core == 0, ahead, behind), (*ctx, 'core'), [(2 * a...  4.27 us
    ppermute x1, starting transfers between devices, local(): other_weight = lax.ppermute(pack(core, weight), 'core', [(0, 1), (1, 0)])  3.53 us
  transfers between devices with their start and end apart: 5, of which 2 were waited for; matrix products, arithmetic and copies ran while one was open for 0% of the time, Pallas kernels for 12%

profile of v4, /device:TPU:1, one launch (start us, length us, event | category | flops | bytes accessed | tf_op | source)
XLA Modules:
  0.0 135.2 jit_solution(6595189432112475734)
XLA Ops:
  6.5 1.8 %stage.1 = (bf16[272,512]{1,0:T(8,128)(2,1)}, bf16[528,128]{1,0:T(8,128)(2,1)}) custom-call(bf16[256,512]{1,0:T(8,128)(2,1)} %q.1, bf16[256,128]{1,0:T(8,128)(2,1)} %k.1, bf16[256,128]{1,0:T(8,128)(2,1)} %v.1, s32[2,128]{1,0:T(2,128)} %bitcast.15), custom_call_target="tpu_custom_call" | custom-call | tf_op jit(solution)/shard_map/stage/pallas_call | solution.py:306
  8.3 0.0 all-gather.5.cloned.1.call-update
  8.3 37.6 %all-gather.1 = bf16[2112,128]{1,0:T(8,128)(2,1)S(1)} all-gather(bf16[528,128]{1,0:T(8,128)(2,1)} %get-tuple-element.14), channel_id=3, replica_groups={{0,160,320,480},{8,168,328,488},{16,176,336,496},{24,184,344,504},{32,1..., dimensions={0}, use_global_device_ids=true | all-gather | bytes 675840 | tf_op jit(solution)/shard_map/all_gather | solution.py:326
  45.9 5.3 %collective-permute-start = (bf16[4,528,128]{2,1,0:T(8,128)(2,1)S(1)}, bf16[4,528,128]{2,1,0:T(8,128)(2,1)S(1)}, u32[]{:S(2)}, u32[]{:S(2)}) collective-permute-start(bf16[4,528,128]{2,1,0:T(8,128)(2,1)S(1)} %bitcast.9), channel_id=1, source_target_pairs={{8,0},{16,8},{24,16},{160,24},{168,160},{176,168},{184,176},{320,1... | collective-permute-start | bytes 1622024 | tf_op jit(solution)/shard_map/ppermute | solution.py:327
  51.2 1.9 %collective-permute-start.1 = (bf16[4,528,128]{2,1,0:T(8,128)(2,1)S(1)}, bf16[4,528,128]{2,1,0:T(8,128)(2,1)S(1)}, u32[]{:S(2)}, u32[]{:S(2)}) collective-permute-start(bf16[4,528,128]{2,1,0:T(8,128)(2,1)S(1)} %bitcast.10), channel_id=1, source_target_pairs={{504,0},{0,8},{8,16},{16,24},{24,160},{160,168},{168,176},{176,184... | collective-permute-start | bytes 1622024 | tf_op jit(solution)/shard_map/ppermute | solution.py:328
  53.1 0.0 all-gather.5.cloned.1.call-done
  53.2 1.2 copy-done.1
  54.4 3.9 %attend.3 = (f32[4,4,144,256]{3,2,1,0:T(8,128)S(1)}, f32[4,4,1,256]{3,2,1,0:T(1,128)S(1)}) custom-call(s32[1]{0:T(128)} %bitcast.1.y_ref, s32[1]{0:T(128)} %bitcast.2.z_ref, bf16[4,272,512]{2,1,0:T(8,128)(2,1)S(1)} %bitcast.12, bf16[4,528,128]{2,1,0:T(8,128)(2,1)S(1)} %bitcast.11), custom_call_target="tpu_custom_call" | custom-call | flops 2684354560 | bytes 6291456 | tf_op jit(solution)/shard_map/attend/pallas_call | solution.py:193
  58.3 0.4 pack.1
  58.8 3.5 %collective-permute-start.3 = (bf16[4,512,512]{2,1,0:T(8,128)(2,1)S(1)}, bf16[4,512,512]{2,1,0:T(8,128)(2,1)S(1)}, u32[]{:S(2)}, u32[]{:S(2)}) collective-permute-start(bf16[4,512,512]{2,1,0:T(8,128)(2,1)S(1)} %pack.1), channel_id=1, source_target_pairs={{0,1},{1,0},{2,3},{3,2},{4,5},{5,4},{6,7},{7,6},{8,9},{9,8},{10,11... | collective-permute-start | bytes 6291464 | tf_op jit(solution)/shard_map/ppermute | solution.py:333
  62.3 0.0 collective-permute-done.refs_0_
  62.3 6.5 %collective-permute-done.1.refs_1_ = bf16[4,528,128]{2,1,0:T(8,128)(2,1)S(1)} collective-permute-done((bf16[4,528,128]{2,1,0:T(8,128)(2,1)S(1)}, bf16[4,528,128]{2,1,0:T(8,128)(2,1)S(1)}, u32[]{:S(2)}, u32[]{:S(2)}) %collective-permute-start.1) | collective-permute-done | bytes 540704 | tf_op jit(solution)/shard_map/ppermute | solution.py:328
  68.8 0.1 broadcast_select_fusion
  68.9 1.9 %collective-permute-start.2 = (bf16[4,528,128]{2,1,0:T(8,128)(2,1)S(1)}, bf16[4,528,128]{2,1,0:T(8,128)(2,1)S(1)}, u32[]{:S(2)}, u32[]{:S(2)}) collective-permute-start(bf16[4,528,128]{2,1,0:T(8,128)(2,1)S(1)} %broadcast_select_fusion), channel_id=1, source_target_pairs={{8,0},{16,8},{24,16},{160,24},{168,160},{176,168},{184,176},{320,1... | collective-permute-start | bytes 1622024 | tf_op jit(solution)/shard_map/ppermute | solution.py:334
  70.8 7.2 %attend.4 = (f32[4,4,144,256]{3,2,1,0:T(8,128)S(1)}, f32[4,4,1,256]{3,2,1,0:T(1,128)S(1)}) custom-call(s32[1]{0:T(128)} %bitcast.1.y_ref, s32[1]{0:T(128)} %bitcast.2.z_ref, bf16[4,272,512]{2,1,0:T(8,128)(2,1)S(1)} %bitcast.13, bf16[4,528,128]{2,1,0:T(8,128)(2,1)S(1)} %collective-permute-done.refs_0_, ...), custom_call_target="tpu_custom_call", output_to_operand_aliasing={{0}: (5, {}), {1}: (6, {})} | custom-call | flops 5368709120 | bytes 6291456 | tf_op jit(solution)/shard_map/attend/pallas_call | solution.py:193
  78.0 4.3 %collective-permute-done.2.refs_0_ = bf16[4,528,128]{2,1,0:T(8,128)(2,1)S(1)} collective-permute-done((bf16[4,528,128]{2,1,0:T(8,128)(2,1)S(1)}, bf16[4,528,128]{2,1,0:T(8,128)(2,1)S(1)}, u32[]{:S(2)}, u32[]{:S(2)}) %collective-permute-start.2) | collective-permute-done | bytes 540704 | tf_op jit(solution)/shard_map/ppermute | solution.py:334
  82.3 4.2 %attend.5 = bf16[4,528,256]{2,1,0:T(8,128)(2,1)S(1)} custom-call(s32[1]{0:T(128)} %bitcast.1.y_ref, s32[1]{0:T(128)} %bitcast.2.z_ref, bf16[4,272,512]{2,1,0:T(8,128)(2,1)S(1)} %bitcast.14, bf16[4,528,128]{2,1,0:T(8,128)(2,1)S(1)} %collective-permute-done.2.refs_0_, f32[4,4,144,256]{3,2,1,0:T(8,128)S(1)} %get-tuple-element.18.refs_1_, ...), custom_call_target="tpu_custom_call" | custom-call | flops 2684354560 | bytes 6291456 | tf_op jit(solution)/shard_map/attend/pallas_call | solution.py:193
  86.5 17.6 %all_to_all.10.parts = bf16[4,528,256]{2,1,0:T(8,128)(2,1)S(1)} all-to-all(bf16[4,528,256]{2,1,0:T(8,128)(2,1)S(1)} %attend.5), channel_id=1, replica_groups=mesh['y'=4,'z'=16,'x'=4,'core'=2] {'y'}, dimensions={0} | all-to-all | bytes 2162688 | tf_op jit(solution)/shard_map/all_to_all | solution.py:341
  104.1 0.3 combine.1
  104.4 3.1 %all-gather.2 = bf16[512,512]{1,0:T(8,128)(2,1)S(1)} all-gather(bf16[256,512]{1,0:T(8,128)(2,1)S(1)} %combine.1), channel_id=4, replica_groups=mesh['y'=4,'z'=16,'x'=4,'core'=2] {'core'}, dimensions={0}, use_global_device_ids=true | all-gather | bytes 786432 | tf_op jit(solution)/shard_map/all_gather | solution.py:342
  107.4 0.0 collective-permute-done.3.other_weight
  107.4 2.0 %project.1 = bf16[4,256,512]{2,1,0:T(8,128)(2,1)S(1)} custom-call(s32[1]{0:T(128)} %bitcast.core, bf16[2,256,512]{2,1,0:T(8,128)(2,1)S(1)} %bitcast.8, bf16[512,4096]{1,0:T(8,128)(2,1)S(1)} %copy-done, bf16[4,512,512]{2,1,0:T(8,128)(2,1)S(1)} %collective-permute-done.3.other_weight), custom_call_target="tpu_custom_call" | custom-call | tf_op jit(solution)/shard_map/project/pallas_call | solution.py:272
  109.4 18.0 %all_to_all.11 = bf16[4,256,512]{2,1,0:T(8,128)(2,1)S(1)} all-to-all(bf16[4,256,512]{2,1,0:T(8,128)(2,1)S(1)} %project.1), channel_id=1, replica_groups=mesh['y'=4,'z'=16,'x'=4,'core'=2] {'x'}, dimensions={0} | all-to-all | bytes 2097152 | tf_op jit(solution)/shard_map/all_to_all | solution.py:344
  127.5 0.9 reduce_sum.12
  (4 shorter events, 0.0 us)
Async XLA Ops:
  6.5 46.6 %all-gather.5.cloned.1.call-start = ((), (), s32[]{:S(2)}) async-start(), calls=%async_computation.2 | async-start | bytes 1392640 | tf_op jit(solution)/shard_map/all_gather | solution.py:325
  45.9 16.4 %collective-permute-start = (bf16[4,528,128]{2,1,0:T(8,128)(2,1)S(1)}, bf16[4,528,128]{2,1,0:T(8,128)(2,1)S(1)}, u32[]{:S(2)}, u32[]{:S(2)}) collective-permute-start(bf16[4,528,128]{2,1,0:T(8,128)(2,1)S(1)} %bitcast.9), channel_id=1, source_target_pairs={{8,0},{16,8},{24,16},{160,24},{168,160},{176,168},{184,176},{320,1... | collective-permute-start | bytes 1622024 | tf_op jit(solution)/shard_map/ppermute | solution.py:327
  51.2 17.6 %collective-permute-start.1 = (bf16[4,528,128]{2,1,0:T(8,128)(2,1)S(1)}, bf16[4,528,128]{2,1,0:T(8,128)(2,1)S(1)}, u32[]{:S(2)}, u32[]{:S(2)}) collective-permute-start(bf16[4,528,128]{2,1,0:T(8,128)(2,1)S(1)} %bitcast.10), channel_id=1, source_target_pairs={{504,0},{0,8},{8,16},{16,24},{24,160},{160,168},{168,176},{176,184... | collective-permute-start | bytes 1622024 | tf_op jit(solution)/shard_map/ppermute | solution.py:328
  53.2 1.2 copy-start.1
  54.4 3.9 %copy-start = (bf16[512,4096]{1,0:T(8,128)(2,1)S(1)}, bf16[512,4096]{1,0:T(8,128)(2,1)}, u32[]{:S(2)}) copy-start(bf16[512,4096]{1,0:T(8,128)(2,1)} %own_weight.1) | copy-start | bytes 12582916
  58.8 48.7 %collective-permute-start.3 = (bf16[4,512,512]{2,1,0:T(8,128)(2,1)S(1)}, bf16[4,512,512]{2,1,0:T(8,128)(2,1)S(1)}, u32[]{:S(2)}, u32[]{:S(2)}) collective-permute-start(bf16[4,512,512]{2,1,0:T(8,128)(2,1)S(1)} %pack.1), channel_id=1, source_target_pairs={{0,1},{1,0},{2,3},{3,2},{4,5},{5,4},{6,7},{7,6},{8,9},{9,8},{10,11... | collective-permute-start | bytes 6291464 | tf_op jit(solution)/shard_map/ppermute | solution.py:333
  68.9 13.4 %collective-permute-start.2 = (bf16[4,528,128]{2,1,0:T(8,128)(2,1)S(1)}, bf16[4,528,128]{2,1,0:T(8,128)(2,1)S(1)}, u32[]{:S(2)}, u32[]{:S(2)}) collective-permute-start(bf16[4,528,128]{2,1,0:T(8,128)(2,1)S(1)} %broadcast_select_fusion), channel_id=1, source_target_pairs={{8,0},{16,8},{24,16},{160,24},{168,160},{176,168},{184,176},{320,1... | collective-permute-start | bytes 1622024 | tf_op jit(solution)/shard_map/ppermute | solution.py:334
Sparse Core Ops, SparseCore 0:
  9.5 38.0 all-gather.4

commit v5 on v4

--- a/solution.py
+++ b/solution.py
@@ -47,6 +47,8 @@
 def attend_kernel(steps, first, last, y_ref, z_ref, q_ref, *refs):
     kinds = len(steps)
     blocks, refs = refs[:kinds], refs[kinds:]
+    y, z = y_ref[0], z_ref[0]
+    d = (z // 4 + 4 - y) % 4
     if first:
         acc_in = max_in = None
     else:
@@ -61,13 +63,16 @@
     def key_block(n, i):
         return blocks[n].at[i]
 
+    def query_block(q):
+        return q_ref.at[(q + 4 - y) % 4]
+
     for n in range(kinds):
         for i in range(4):
             v_buf[n, i, 0:HEAD, :] = key_block(n, i)[TOK : 2 * TOK, :].T
             v_buf[n, i, HEAD:VROWS, :] = jnp.ones((16, TOK), BF16)
 
     def query(q, h):
-        return q_ref[q, 0:TOK, pl.ds(pl.multiple_of(h * HEAD, HEAD), HEAD)]
+        return query_block(q)[0:TOK, pl.ds(pl.multiple_of(h * HEAD, HEAD), HEAD)]
 
     def score(q, h, n, i):
         return dot(key_block(n, i)[0:TOK, :], query(q, h), ((1,), (1,)))
@@ -132,7 +137,7 @@
             line = rows[half : half + 1, :] * 32.0 + rows[half + 2 : half + 3, :]
             key_ids.append(jnp.broadcast_to(line, (128, 128)).T)
         key_ids = jnp.concatenate(key_ids, axis=0)
-        tail = q_ref[q, TOK : TOK + 16, :].astype(F32)
+        tail = query_block(q)[TOK : TOK + 16, :].astype(F32)
         query_ids = (tail[:, 0:TOK] * 32.0 + tail[:, TOK : 2 * TOK])[0:1, :]
         seen = jnp.concatenate([key_ids, key_ids], axis=1) <= query_ids
         s = score(q, 0, n, i)
@@ -148,8 +153,6 @@
             row_max[q, h] = new
             s = s_next
 
-    y, z = y_ref[0], z_ref[0]
-    d = (z // 4 + 4 - y) % 4
     for n, step in enumerate(steps):
         kind = (z + step + 4) % 4
         count = jnp.minimum((z + 5 - kind) // 4, 4)
@@ -322,11 +325,14 @@
     core = lax.axis_index("core").reshape(1)
 
     staged, block = stage(queries, keys, values, block_ids.reshape(2, 128))
-    q_all = lax.all_gather(staged, "y", axis=0)
+    q_others = [
+        lax.ppermute(staged, "y", [((i + n) % NY, i) for i in range(NY)]) for n in (1, 2, 3)
+    ]
     own = lax.all_gather(block, ctx, axis=0, axis_index_groups=ring_groups())
     ahead = lax.ppermute(own, ctx, ring_step(1))
     behind = lax.ppermute(own, ctx, ring_step(-1))
 
+    q_all = jnp.stack([staged, *q_others])
     state = attend((0,), True, False, place, q_all, [own], ())
     weight, row_max = lax.optimization_barrier((out_weight, state[1]))
     state = (state[0], row_max)

time: 136 us -> 127 us (0.934)
  between operations: 13.5 us -> 0.18 us
  starting transfers between devices: 12.6 us -> 23.4 us
  waiting for transfers between devices: 10.8 us -> 6.44 us
  blocking collectives: 76.2 us -> 74.7 us
    ppermute x0 -> x3, starting transfers between devices: none -> 10.3 us  [local(): lax.ppermute(staged, 'y', [((i + n) % NY, i) for i in range(NY)])]
    ppermute x1, waiting for transfers between devices: 6.5 us -> 0.01 us  [local(): behind = lax.ppermute(own, ctx, ring_step(-1))]
    ppermute x1, starting transfers between devices: 5.28 us -> 1.91 us  [local(): ahead = lax.ppermute(own, ctx, ring_step(1))]
    ppermute x1, starting transfers between devices: 3.53 us -> 5.93 us  [local(): other_weight = lax.ppermute(pack(core, weight), 'core', [(0, 1), (1, 0)])]
    ppermute x1, waiting for transfers between devices: 4.27 us -> 6.42 us  [local(): lax.ppermute(jnp.where(core == 0, ahead, behind), (*ctx, 'core'), [(2 * a...]
    all_gather x1, blocking collectives: 37.6 us -> 36 us  [local(): own = lax.all_gather(block, ctx, axis=0, axis_index_groups=ring_groups())]
    ppermute x1, starting transfers between devices: 1.92 us -> 3.36 us  [local(): behind = lax.ppermute(own, ctx, ring_step(-1))]
  transfers between devices with their start and end apart: 5 -> 7, of which waited for: 2 -> 1; matrix products, arithmetic and copies ran while one was open for 0% -> 1% of each run, Pallas kernels for 12% -> 13%
where the time goes in v5:
time: 127 us
  blocking collectives  74.7 us (59%)
  starting transfers between devices  23.4 us (18%)
  Pallas kernels  19.9 us (16%)
  waiting for transfers between devices  6.44 us (5%)
  other arithmetic  2.06 us (2%)
    all_gather x1, blocking collectives, local(): own = lax.all_gather(block, ctx, axis=0, axis_index_groups=ring_groups())  36 us
    all_to_all x1, blocking collectives, local(): shares = lax.all_to_all(share, 'x', 0, 0, tiled=True)  18.1 us
    all_to_all x1, blocking collectives, local(): partial = lax.all_to_all(partial, 'y', 0, 0, tiled=True)  16.8 us
    pallas_call x3, Pallas kernels, attend(): pl.pallas_call(functools.partial(attend_kernel, steps, first, last), out_...  15.4 us
    ppermute x3, starting transfers between devices, local(): lax.ppermute(staged, 'y', [((i + n) % NY, i) for i in range(NY)])  10.3 us
    ppermute x1, waiting for transfers between devices, local(): lax.ppermute(jnp.where(core == 0, ahead, behind), (*ctx, 'core'), [(2 * a...  6.42 us
    ppermute x1, starting transfers between devices, local(): other_weight = lax.ppermute(pack(core, weight), 'core', [(0, 1), (1, 0)])  5.93 us
    all_gather x1, blocking collectives, local(): both = lax.all_gather(combine(partial), 'core', axis=0)  3.82 us
  transfers between devices with their start and end apart: 7, of which 1 were waited for; matrix products, arithmetic and copies ran while one was open for 1% of the time, Pallas kernels for 13%

profile of v5, /device:TPU:1, one launch (start us, length us, event | category | flops | bytes accessed | tf_op | source)
XLA Modules:
  0.0 126.7 jit_solution(846973493872755519)
XLA Ops:
  0.0 1.8 %stage.1 = (bf16[272,512]{1,0:T(8,128)(2,1)}, bf16[528,128]{1,0:T(8,128)(2,1)}) custom-call(bf16[256,512]{1,0:T(8,128)(2,1)} %q.1, bf16[256,128]{1,0:T(8,128)(2,1)} %k.1, bf16[256,128]{1,0:T(8,128)(2,1)} %v.1, s32[2,128]{1,0:T(2,128)} %bitcast.19), custom_call_target="tpu_custom_call" | custom-call | tf_op jit(solution)/shard_map/stage/pallas_call | solution.py:309
  1.8 5.5 %collective-permute-start = (bf16[272,512]{1,0:T(8,128)(2,1)}, bf16[272,512]{1,0:T(8,128)(2,1)S(1)}, u32[]{:S(2)}, u32[]{:S(2)}) collective-permute-start(bf16[272,512]{1,0:T(8,128)(2,1)} %get-tuple-element.13), channel_id=1, source_target_pairs={{128,0},{256,128},{384,256},{0,384},{129,1},{257,129},{385,257},{1... | collective-permute-start | bytes 835592 | tf_op jit(solution)/shard_map/ppermute | solution.py:329
  7.2 2.3 %collective-permute-start.1 = (bf16[272,512]{1,0:T(8,128)(2,1)}, bf16[272,512]{1,0:T(8,128)(2,1)S(1)}, u32[]{:S(2)}, u32[]{:S(2)}) collective-permute-start(bf16[272,512]{1,0:T(8,128)(2,1)} %get-tuple-element.13), channel_id=1, source_target_pairs={{256,0},{384,128},{0,256},{128,384},{257,1},{385,129},{1,257},{129... | collective-permute-start | bytes 835592 | tf_op jit(solution)/shard_map/ppermute | solution.py:329
  9.5 2.6 %collective-permute-start.2 = (bf16[272,512]{1,0:T(8,128)(2,1)}, bf16[272,512]{1,0:T(8,128)(2,1)S(1)}, u32[]{:S(2)}, u32[]{:S(2)}) collective-permute-start(bf16[272,512]{1,0:T(8,128)(2,1)} %get-tuple-element.13), channel_id=1, source_target_pairs={{384,0},{0,128},{128,256},{256,384},{385,1},{1,129},{129,257},{257... | collective-permute-start | bytes 835592 | tf_op jit(solution)/shard_map/ppermute | solution.py:329
  12.1 36.0 %all-gather = bf16[2112,128]{1,0:T(8,128)(2,1)S(1)} all-gather(bf16[528,128]{1,0:T(8,128)(2,1)} %get-tuple-element.14), channel_id=2, replica_groups={{0,160,320,480},{8,168,328,488},{16,176,336,496},{24,184,344,504},{32,1..., dimensions={0}, use_global_device_ids=true | all-gather | bytes 675840 | tf_op jit(solution)/shard_map/all_gather | solution.py:331
  48.1 1.9 %collective-permute-start.3 = (bf16[4,528,128]{2,1,0:T(8,128)(2,1)S(1)}, bf16[4,528,128]{2,1,0:T(8,128)(2,1)S(1)}, u32[]{:S(2)}, u32[]{:S(2)}) collective-permute-start(bf16[4,528,128]{2,1,0:T(8,128)(2,1)S(1)} %bitcast.12), channel_id=1, source_target_pairs={{8,0},{16,8},{24,16},{160,24},{168,160},{176,168},{184,176},{320,1... | collective-permute-start | bytes 1622024 | tf_op jit(solution)/shard_map/ppermute | solution.py:332
  50.0 3.4 %collective-permute-start.4 = (bf16[4,528,128]{2,1,0:T(8,128)(2,1)S(1)}, bf16[4,528,128]{2,1,0:T(8,128)(2,1)S(1)}, u32[]{:S(2)}, u32[]{:S(2)}) collective-permute-start(bf16[4,528,128]{2,1,0:T(8,128)(2,1)S(1)} %bitcast.13), channel_id=1, source_target_pairs={{504,0},{0,8},{8,16},{16,24},{24,160},{160,168},{168,176},{176,184... | collective-permute-start | bytes 1622024 | tf_op jit(solution)/shard_map/ppermute | solution.py:333
  53.4 0.0 collective-permute-done
  53.4 1.1 pad_maximum_fusion.q_ref
  54.5 0.0 copy-start
  54.6 3.9 %attend.3 = (f32[4,4,144,256]{3,2,1,0:T(8,128)S(1)}, f32[4,4,1,256]{3,2,1,0:T(1,128)S(1)}) custom-call(s32[1]{0:T(128)} %bitcast.1.y_ref, s32[1]{0:T(128)} %bitcast.2.z_ref, bf16[4,272,512]{2,1,0:T(8,128)(2,1)S(1)} %pad_maximum_fusion.q_ref, bf16[4,528,128]{2,1,0:T(8,128)(2,1)S(1)} %bitcast.14), custom_call_target="tpu_custom_call" | custom-call | flops 2684354560 | bytes 6291456 | tf_op jit(solution)/shard_map/attend/pallas_call | solution.py:196
  58.5 0.4 pack.1
  58.9 5.9 %collective-permute-start.6 = (bf16[4,512,512]{2,1,0:T(8,128)(2,1)S(1)}, bf16[4,512,512]{2,1,0:T(8,128)(2,1)S(1)}, u32[]{:S(2)}, u32[]{:S(2)}) collective-permute-start(bf16[4,512,512]{2,1,0:T(8,128)(2,1)S(1)} %pack.1), channel_id=1, source_target_pairs={{0,1},{1,0},{2,3},{3,2},{4,5},{5,4},{6,7},{7,6},{8,9},{9,8},{10,11... | collective-permute-start | bytes 6291464 | tf_op jit(solution)/shard_map/ppermute | solution.py:339
  64.9 0.1 broadcast_select_fusion
  65.0 1.9 %collective-permute-start.5 = (bf16[4,528,128]{2,1,0:T(8,128)(2,1)S(1)}, bf16[4,528,128]{2,1,0:T(8,128)(2,1)S(1)}, u32[]{:S(2)}, u32[]{:S(2)}) collective-permute-start(bf16[4,528,128]{2,1,0:T(8,128)(2,1)S(1)} %broadcast_select_fusion), channel_id=1, source_target_pairs={{8,0},{16,8},{24,16},{160,24},{168,160},{176,168},{184,176},{320,1... | collective-permute-start | bytes 1622024 | tf_op jit(solution)/shard_map/ppermute | solution.py:340
  66.9 7.2 %attend.4 = (f32[4,4,144,256]{3,2,1,0:T(8,128)S(1)}, f32[4,4,1,256]{3,2,1,0:T(1,128)S(1)}) custom-call(s32[1]{0:T(128)} %bitcast.1.y_ref, s32[1]{0:T(128)} %bitcast.2.z_ref, bf16[4,272,512]{2,1,0:T(8,128)(2,1)S(1)} %pad_maximum_fusion.q_ref, bf16[4,528,128]{2,1,0:T(8,128)(2,1)S(1)} %collective-permute-done.3.refs_0_, ...), custom_call_target="tpu_custom_call", output_to_operand_aliasing={{0}: (5, {}), {1}: (6, {})} | custom-call | flops 5368709120 | bytes 6291456 | tf_op jit(solution)/shard_map/attend/pallas_call | solution.py:196
  74.2 6.4 %collective-permute-done.5.refs_0_ = bf16[4,528,128]{2,1,0:T(8,128)(2,1)S(1)} collective-permute-done((bf16[4,528,128]{2,1,0:T(8,128)(2,1)S(1)}, bf16[4,528,128]{2,1,0:T(8,128)(2,1)S(1)}, u32[]{:S(2)}, u32[]{:S(2)}) %collective-permute-start.5) | collective-permute-done | bytes 540704 | tf_op jit(solution)/shard_map/ppermute | solution.py:340
  80.6 4.3 %attend.5 = bf16[4,528,256]{2,1,0:T(8,128)(2,1)S(1)} custom-call(s32[1]{0:T(128)} %bitcast.1.y_ref, s32[1]{0:T(128)} %bitcast.2.z_ref, bf16[4,272,512]{2,1,0:T(8,128)(2,1)S(1)} %pad_maximum_fusion.q_ref, bf16[4,528,128]{2,1,0:T(8,128)(2,1)S(1)} %collective-permute-done.5.refs_0_, f32[4,4,144,256]{3,2,1,0:T(8,128)S(1)} %get-tuple-element.18.refs_1_, ...), custom_call_target="tpu_custom_call" | custom-call | flops 2684354560 | bytes 6291456 | tf_op jit(solution)/shard_map/attend/pallas_call | solution.py:196
  84.8 16.8 %all_to_all.10.parts = bf16[4,528,256]{2,1,0:T(8,128)(2,1)S(1)} all-to-all(bf16[4,528,256]{2,1,0:T(8,128)(2,1)S(1)} %attend.5), channel_id=1, replica_groups=mesh['y'=4,'z'=16,'x'=4,'core'=2] {'y'}, dimensions={0} | all-to-all | bytes 2162688 | tf_op jit(solution)/shard_map/all_to_all | solution.py:347
  101.6 0.3 combine.1
  101.9 3.8 %all-gather.1 = bf16[512,512]{1,0:T(8,128)(2,1)S(1)} all-gather(bf16[256,512]{1,0:T(8,128)(2,1)S(1)} %combine.1), channel_id=3, replica_groups=mesh['y'=4,'z'=16,'x'=4,'core'=2] {'core'}, dimensions={0}, use_global_device_ids=true | all-gather | bytes 786432 | tf_op jit(solution)/shard_map/all_gather | solution.py:348
  105.7 2.0 %project.1 = bf16[4,256,512]{2,1,0:T(8,128)(2,1)S(1)} custom-call(s32[1]{0:T(128)} %bitcast.core, bf16[2,256,512]{2,1,0:T(8,128)(2,1)S(1)} %bitcast.11, bf16[512,4096]{1,0:T(8,128)(2,1)S(1)} %copy-done, bf16[4,512,512]{2,1,0:T(8,128)(2,1)S(1)} %collective-permute-done.6.other_weight), custom_call_target="tpu_custom_call" | custom-call | tf_op jit(solution)/shard_map/project/pallas_call | solution.py:275
  107.7 18.1 %all_to_all.11 = bf16[4,256,512]{2,1,0:T(8,128)(2,1)S(1)} all-to-all(bf16[4,256,512]{2,1,0:T(8,128)(2,1)S(1)} %project.1), channel_id=1, replica_groups=mesh['y'=4,'z'=16,'x'=4,'core'=2] {'x'}, dimensions={0} | all-to-all | bytes 2097152 | tf_op jit(solution)/shard_map/all_to_all | solution.py:350
  125.8 0.9 reduce_sum.12
  (6 shorter events, 0.0 us)
Async XLA Ops:
  1.8 51.7 %collective-permute-start = (bf16[272,512]{1,0:T(8,128)(2,1)}, bf16[272,512]{1,0:T(8,128)(2,1)S(1)}, u32[]{:S(2)}, u32[]{:S(2)}) collective-permute-start(bf16[272,512]{1,0:T(8,128)(2,1)} %get-tuple-element.13), channel_id=1, source_target_pairs={{128,0},{256,128},{384,256},{0,384},{129,1},{257,129},{385,257},{1... | collective-permute-start | bytes 835592 | tf_op jit(solution)/shard_map/ppermute | solution.py:329
  7.2 46.2 %collective-permute-start.1 = (bf16[272,512]{1,0:T(8,128)(2,1)}, bf16[272,512]{1,0:T(8,128)(2,1)S(1)}, u32[]{:S(2)}, u32[]{:S(2)}) collective-permute-start(bf16[272,512]{1,0:T(8,128)(2,1)} %get-tuple-element.13), channel_id=1, source_target_pairs={{256,0},{384,128},{0,256},{128,384},{257,1},{385,129},{1,257},{129... | collective-permute-start | bytes 835592 | tf_op jit(solution)/shard_map/ppermute | solution.py:329
  9.5 43.9 %collective-permute-start.2 = (bf16[272,512]{1,0:T(8,128)(2,1)}, bf16[272,512]{1,0:T(8,128)(2,1)S(1)}, u32[]{:S(2)}, u32[]{:S(2)}) collective-permute-start(bf16[272,512]{1,0:T(8,128)(2,1)} %get-tuple-element.13), channel_id=1, source_target_pairs={{384,0},{0,128},{128,256},{256,384},{385,1},{1,129},{129,257},{257... | collective-permute-start | bytes 835592 | tf_op jit(solution)/shard_map/ppermute | solution.py:329
  48.1 16.8 %collective-permute-start.3 = (bf16[4,528,128]{2,1,0:T(8,128)(2,1)S(1)}, bf16[4,528,128]{2,1,0:T(8,128)(2,1)S(1)}, u32[]{:S(2)}, u32[]{:S(2)}) collective-permute-start(bf16[4,528,128]{2,1,0:T(8,128)(2,1)S(1)} %bitcast.12), channel_id=1, source_target_pairs={{8,0},{16,8},{24,16},{160,24},{168,160},{176,168},{184,176},{320,1... | collective-permute-start | bytes 1622024 | tf_op jit(solution)/shard_map/ppermute | solution.py:332
  50.0 14.9 %collective-permute-start.4 = (bf16[4,528,128]{2,1,0:T(8,128)(2,1)S(1)}, bf16[4,528,128]{2,1,0:T(8,128)(2,1)S(1)}, u32[]{:S(2)}, u32[]{:S(2)}) collective-permute-start(bf16[4,528,128]{2,1,0:T(8,128)(2,1)S(1)} %bitcast.13), channel_id=1, source_target_pairs={{504,0},{0,8},{8,16},{16,24},{24,160},{160,168},{168,176},{176,184... | collective-permute-start | bytes 1622024 | tf_op jit(solution)/shard_map/ppermute | solution.py:333
  54.5 4.0 %copy-start = (bf16[512,4096]{1,0:T(8,128)(2,1)S(1)}, bf16[512,4096]{1,0:T(8,128)(2,1)}, u32[]{:S(2)}) copy-start(bf16[512,4096]{1,0:T(8,128)(2,1)} %own_weight.1) | copy-start | bytes 12582916
  58.9 46.8 %collective-permute-start.6 = (bf16[4,512,512]{2,1,0:T(8,128)(2,1)S(1)}, bf16[4,512,512]{2,1,0:T(8,128)(2,1)S(1)}, u32[]{:S(2)}, u32[]{:S(2)}) collective-permute-start(bf16[4,512,512]{2,1,0:T(8,128)(2,1)S(1)} %pack.1), channel_id=1, source_target_pairs={{0,1},{1,0},{2,3},{3,2},{4,5},{5,4},{6,7},{7,6},{8,9},{9,8},{10,11... | collective-permute-start | bytes 6291464 | tf_op jit(solution)/shard_map/ppermute | solution.py:339
  65.0 15.6 %collective-permute-start.5 = (bf16[4,528,128]{2,1,0:T(8,128)(2,1)S(1)}, bf16[4,528,128]{2,1,0:T(8,128)(2,1)S(1)}, u32[]{:S(2)}, u32[]{:S(2)}) collective-permute-start(bf16[4,528,128]{2,1,0:T(8,128)(2,1)S(1)} %broadcast_select_fusion), channel_id=1, source_target_pairs={{8,0},{16,8},{24,16},{160,24},{168,160},{176,168},{184,176},{320,1... | collective-permute-start | bytes 1622024 | tf_op jit(solution)/shard_map/ppermute | solution.py:340

commit v6 on v5

--- a/solution.py
+++ b/solution.py
@@ -334,16 +334,17 @@
 
     q_all = jnp.stack([staged, *q_others])
     state = attend((0,), True, False, place, q_all, [own], ())
-    weight, row_max = lax.optimization_barrier((out_weight, state[1]))
+    sent, row_max = lax.optimization_barrier((jnp.where(core == 0, ahead, behind), state[1]))
     state = (state[0], row_max)
-    other_weight = lax.ppermute(pack(core, weight), "core", [(0, 1), (1, 0)])
     far = lax.ppermute(
-        jnp.where(core == 0, ahead, behind),
+        sent,
         (*ctx, "core"),
         [(2 * a + c, 2 * b + c) for c in range(2) for a, b in ring_step(1 - 2 * c)],
     )
     state = attend((1, -1), False, False, place, q_all, [ahead, behind], state)
     partial = attend((2,), False, True, place, q_all, [far], state)
+    weight, partial = lax.optimization_barrier((out_weight, partial))
+    other_weight = lax.ppermute(pack(core, weight), "core", [(0, 1), (1, 0)])
     partial = lax.all_to_all(partial, "y", 0, 0, tiled=True)
     both = lax.all_gather(combine(partial), "core", axis=0)
     share = project(core, both, out_weight, other_weight)

time: 127 us -> 131 us (1.031)
  waiting for transfers between devices: 6.44 us -> 10.4 us
  blocking collectives: 74.7 us -> 72.1 us
  starting transfers between devices: 23.4 us -> 25.7 us
    all_gather x1, blocking collectives: 36 us -> 32.6 us  [local(): own = lax.all_gather(block, ctx, axis=0, axis_index_groups=ring_groups())]
    ppermute x1, waiting for transfers between devices: 0.01 us -> 3.36 us  [local(): behind = lax.ppermute(own, ctx, ring_step(-1))]
    ppermute x1, waiting for transfers between devices: 0.01 us -> 2.76 us  [local(): ahead = lax.ppermute(own, ctx, ring_step(1))]
    ppermute x1, waiting for transfers between devices: 6.42 us -> 4.24 us  [local(): lax.ppermute(sent, (*ctx, 'core'), [(2 * a + c, 2 * b + c) for c in range...]
    all_to_all x1, blocking collectives: 16.8 us -> 18.2 us  [local(): partial = lax.all_to_all(partial, 'y', 0, 0, tiled=True)]
  transfers between devices with their start and end apart: 7 -> 7, of which waited for: 1 -> 3; matrix products, arithmetic and copies ran while one was open for 1% -> 1% of each run, Pallas kernels for 13% -> 9%
where the time goes in v6:
time: 131 us; the launch traced here: 130 us
  blocking collectives  72.1 us (55%)
  starting transfers between devices  25.7 us (20%)
  Pallas kernels  19.9 us (15%)
  waiting for transfers between devices  10.4 us (8%)
  other arithmetic  2.06 us (2%)
    all_gather x1, blocking collectives, local(): own = lax.all_gather(block, ctx, axis=0, axis_index_groups=ring_groups())  32.6 us
    all_to_all x1, blocking collectives, local(): partial = lax.all_to_all(partial, 'y', 0, 0, tiled=True)  18.2 us
    all_to_all x1, blocking collectives, local(): shares = lax.all_to_all(share, 'x', 0, 0, tiled=True)  18 us
    pallas_call x3, Pallas kernels, attend(): pl.pallas_call(functools.partial(attend_kernel, steps, first, last), out_...  15.4 us
    ppermute x3, starting transfers between devices, local(): lax.ppermute(staged, 'y', [((i + n) % NY, i) for i in range(NY)])  11.5 us
    ppermute x1, starting transfers between devices, local(): other_weight = lax.ppermute(pack(core, weight), 'core', [(0, 1), (1, 0)])  6.93 us
    ppermute x1, waiting for transfers between devices, local(): lax.ppermute(sent, (*ctx, 'core'), [(2 * a + c, 2 * b + c) for c in range...  4.24 us
    ppermute x1, waiting for transfers between devices, local(): behind = lax.ppermute(own, ctx, ring_step(-1))  3.36 us
  transfers between devices with their start and end apart: 7, of which 3 were waited for; matrix products, arithmetic and copies ran while one was open for 1% of the time, Pallas kernels for 9%

profile of v6, /device:TPU:1, one launch (start us, length us, event | category | flops | bytes accessed | tf_op | source)
XLA Modules:
  0.0 130.2 jit_solution(8609193518323680130)
XLA Ops:
  0.0 1.8 %stage.1 = (bf16[272,512]{1,0:T(8,128)(2,1)}, bf16[528,128]{1,0:T(8,128)(2,1)}) custom-call(bf16[256,512]{1,0:T(8,128)(2,1)} %q.1, bf16[256,128]{1,0:T(8,128)(2,1)} %k.1, bf16[256,128]{1,0:T(8,128)(2,1)} %v.1, s32[2,128]{1,0:T(2,128)} %bitcast.19), custom_call_target="tpu_custom_call" | custom-call | tf_op jit(solution)/shard_map/stage/pallas_call | solution.py:309
  1.8 4.0 %collective-permute-start.2 = (bf16[272,512]{1,0:T(8,128)(2,1)}, bf16[272,512]{1,0:T(8,128)(2,1)S(1)}, u32[]{:S(2)}, u32[]{:S(2)}) collective-permute-start(bf16[272,512]{1,0:T(8,128)(2,1)} %get-tuple-element.15), channel_id=1, source_target_pairs={{384,0},{0,128},{128,256},{256,384},{385,1},{1,129},{129,257},{257... | collective-permute-start | bytes 835592 | tf_op jit(solution)/shard_map/ppermute | solution.py:329
  5.8 4.5 %collective-permute-start.1 = (bf16[272,512]{1,0:T(8,128)(2,1)}, bf16[272,512]{1,0:T(8,128)(2,1)S(1)}, u32[]{:S(2)}, u32[]{:S(2)}) collective-permute-start(bf16[272,512]{1,0:T(8,128)(2,1)} %get-tuple-element.15), channel_id=1, source_target_pairs={{256,0},{384,128},{0,256},{128,384},{257,1},{385,129},{1,257},{129... | collective-permute-start | bytes 835592 | tf_op jit(solution)/shard_map/ppermute | solution.py:329
  10.3 3.0 %collective-permute-start = (bf16[272,512]{1,0:T(8,128)(2,1)}, bf16[272,512]{1,0:T(8,128)(2,1)S(1)}, u32[]{:S(2)}, u32[]{:S(2)}) collective-permute-start(bf16[272,512]{1,0:T(8,128)(2,1)} %get-tuple-element.15), channel_id=1, source_target_pairs={{128,0},{256,128},{384,256},{0,384},{129,1},{257,129},{385,257},{1... | collective-permute-start | bytes 835592 | tf_op jit(solution)/shard_map/ppermute | solution.py:329
  13.3 32.6 %all-gather = bf16[2112,128]{1,0:T(8,128)(2,1)S(1)} all-gather(bf16[528,128]{1,0:T(8,128)(2,1)} %get-tuple-element.16), channel_id=2, replica_groups={{0,160,320,480},{8,168,328,488},{16,176,336,496},{24,184,344,504},{32,1..., dimensions={0}, use_global_device_ids=true | all-gather | bytes 675840 | tf_op jit(solution)/shard_map/all_gather | solution.py:331
  45.9 3.1 %collective-permute-start.3 = (bf16[4,528,128]{2,1,0:T(8,128)(2,1)S(1)}, bf16[4,528,128]{2,1,0:T(8,128)(2,1)S(1)}, u32[]{:S(2)}, u32[]{:S(2)}) collective-permute-start(bf16[4,528,128]{2,1,0:T(8,128)(2,1)S(1)} %bitcast.12), channel_id=1, source_target_pairs={{8,0},{16,8},{24,16},{160,24},{168,160},{176,168},{184,176},{320,1... | collective-permute-start | bytes 1622024 | tf_op jit(solution)/shard_map/ppermute | solution.py:332
  49.0 2.2 %collective-permute-start.4 = (bf16[4,528,128]{2,1,0:T(8,128)(2,1)S(1)}, bf16[4,528,128]{2,1,0:T(8,128)(2,1)S(1)}, u32[]{:S(2)}, u32[]{:S(2)}) collective-permute-start(bf16[4,528,128]{2,1,0:T(8,128)(2,1)S(1)} %bitcast.13), channel_id=1, source_target_pairs={{504,0},{0,8},{8,16},{16,24},{24,160},{160,168},{168,176},{176,184... | collective-permute-start | bytes 1622024 | tf_op jit(solution)/shard_map/ppermute | solution.py:333
  51.3 1.1 pad_maximum_fusion.q_ref
  52.4 3.9 %attend.3 = (f32[4,4,144,256]{3,2,1,0:T(8,128)S(1)}, f32[4,4,1,256]{3,2,1,0:T(1,128)S(1)}) custom-call(s32[1]{0:T(128)} %bitcast.1.y_ref, s32[1]{0:T(128)} %bitcast.2.z_ref, bf16[4,272,512]{2,1,0:T(8,128)(2,1)S(1)} %pad_maximum_fusion.q_ref, bf16[4,528,128]{2,1,0:T(8,128)(2,1)S(1)} %bitcast.14), custom_call_target="tpu_custom_call" | custom-call | flops 2684354560 | bytes 6291456 | tf_op jit(solution)/shard_map/attend/pallas_call | solution.py:196
  56.3 2.8 %collective-permute-done.3.refs_0_ = bf16[4,528,128]{2,1,0:T(8,128)(2,1)S(1)} collective-permute-done((bf16[4,528,128]{2,1,0:T(8,128)(2,1)S(1)}, bf16[4,528,128]{2,1,0:T(8,128)(2,1)S(1)}, u32[]{:S(2)}, u32[]{:S(2)}) %collective-permute-start.3) | collective-permute-done | bytes 540704 | tf_op jit(solution)/shard_map/ppermute | solution.py:332
  59.1 3.4 %collective-permute-done.4.refs_1_ = bf16[4,528,128]{2,1,0:T(8,128)(2,1)S(1)} collective-permute-done((bf16[4,528,128]{2,1,0:T(8,128)(2,1)S(1)}, bf16[4,528,128]{2,1,0:T(8,128)(2,1)S(1)}, u32[]{:S(2)}, u32[]{:S(2)}) %collective-permute-start.4) | collective-permute-done | bytes 540704 | tf_op jit(solution)/shard_map/ppermute | solution.py:333
  62.5 0.1 broadcast_select_fusion
  62.5 1.9 %collective-permute-start.5 = (bf16[4,528,128]{2,1,0:T(8,128)(2,1)S(1)}, bf16[4,528,128]{2,1,0:T(8,128)(2,1)S(1)}, u32[]{:S(2)}, u32[]{:S(2)}) collective-permute-start(bf16[4,528,128]{2,1,0:T(8,128)(2,1)S(1)} %broadcast_select_fusion), channel_id=1, source_target_pairs={{8,0},{16,8},{24,16},{160,24},{168,160},{176,168},{184,176},{320,1... | collective-permute-start | bytes 1622024 | tf_op jit(solution)/shard_map/ppermute | solution.py:339
  64.4 7.2 %attend.4 = (f32[4,4,144,256]{3,2,1,0:T(8,128)S(1)}, f32[4,4,1,256]{3,2,1,0:T(1,128)S(1)}) custom-call(s32[1]{0:T(128)} %bitcast.1.y_ref, s32[1]{0:T(128)} %bitcast.2.z_ref, bf16[4,272,512]{2,1,0:T(8,128)(2,1)S(1)} %pad_maximum_fusion.q_ref, bf16[4,528,128]{2,1,0:T(8,128)(2,1)S(1)} %collective-permute-done.3.refs_0_, ...), custom_call_target="tpu_custom_call", output_to_operand_aliasing={{0}: (5, {}), {1}: (6, {})} | custom-call | flops 5368709120 | bytes 6291456 | tf_op jit(solution)/shard_map/attend/pallas_call | solution.py:196
  71.7 4.2 %collective-permute-done.5.refs_0_ = bf16[4,528,128]{2,1,0:T(8,128)(2,1)S(1)} collective-permute-done((bf16[4,528,128]{2,1,0:T(8,128)(2,1)S(1)}, bf16[4,528,128]{2,1,0:T(8,128)(2,1)S(1)}, u32[]{:S(2)}, u32[]{:S(2)}) %collective-permute-start.5) | collective-permute-done | bytes 540704 | tf_op jit(solution)/shard_map/ppermute | solution.py:339
  75.9 4.2 %attend.5 = bf16[4,528,256]{2,1,0:T(8,128)(2,1)S(1)} custom-call(s32[1]{0:T(128)} %bitcast.1.y_ref, s32[1]{0:T(128)} %bitcast.2.z_ref, bf16[4,272,512]{2,1,0:T(8,128)(2,1)S(1)} %pad_maximum_fusion.q_ref, bf16[4,528,128]{2,1,0:T(8,128)(2,1)S(1)} %collective-permute-done.5.refs_0_, f32[4,4,144,256]{3,2,1,0:T(8,128)S(1)} %get-tuple-element.21.refs_1_, ...), custom_call_target="tpu_custom_call" | custom-call | flops 2684354560 | bytes 6291456 | tf_op jit(solution)/shard_map/attend/pallas_call | solution.py:196
  80.2 0.4 pack.1
  80.6 6.9 %collective-permute-start.6 = (bf16[4,512,512]{2,1,0:T(8,128)(2,1)S(1)}, bf16[4,512,512]{2,1,0:T(8,128)(2,1)S(1)}, u32[]{:S(2)}, u32[]{:S(2)}) collective-permute-start(bf16[4,512,512]{2,1,0:T(8,128)(2,1)S(1)} %pack.1), channel_id=1, source_target_pairs={{0,1},{1,0},{2,3},{3,2},{4,5},{5,4},{6,7},{7,6},{8,9},{9,8},{10,11... | collective-permute-start | bytes 6291464 | tf_op jit(solution)/shard_map/ppermute | solution.py:347
  87.6 18.2 %all_to_all.10.parts = bf16[4,528,256]{2,1,0:T(8,128)(2,1)S(1)} all-to-all(bf16[4,528,256]{2,1,0:T(8,128)(2,1)S(1)} %attend.5), channel_id=1, replica_groups=mesh['y'=4,'z'=16,'x'=4,'core'=2] {'y'}, dimensions={0} | all-to-all | bytes 2162688 | tf_op jit(solution)/shard_map/all_to_all | solution.py:348
  105.7 0.3 combine.1
  106.0 3.2 %all-gather.1 = bf16[512,512]{1,0:T(8,128)(2,1)S(1)} all-gather(bf16[256,512]{1,0:T(8,128)(2,1)S(1)} %combine.1), channel_id=3, replica_groups=mesh['y'=4,'z'=16,'x'=4,'core'=2] {'core'}, dimensions={0}, use_global_device_ids=true | all-gather | bytes 786432 | tf_op jit(solution)/shard_map/all_gather | solution.py:349
  109.3 2.0 %project.1 = bf16[4,256,512]{2,1,0:T(8,128)(2,1)S(1)} custom-call(s32[1]{0:T(128)} %bitcast.core, bf16[2,256,512]{2,1,0:T(8,128)(2,1)S(1)} %bitcast.11, bf16[512,4096]{1,0:T(8,128)(2,1)S(1)} %copy-done, bf16[4,512,512]{2,1,0:T(8,128)(2,1)S(1)} %collective-permute-done.6.other_weight), custom_call_target="tpu_custom_call" | custom-call | tf_op jit(solution)/shard_map/project/pallas_call | solution.py:275
  111.2 18.0 %all_to_all.11 = bf16[4,256,512]{2,1,0:T(8,128)(2,1)S(1)} all-to-all(bf16[4,256,512]{2,1,0:T(8,128)(2,1)S(1)} %project.1), channel_id=1, replica_groups=mesh['y'=4,'z'=16,'x'=4,'core'=2] {'x'}, dimensions={0} | all-to-all | bytes 2097152 | tf_op jit(solution)/shard_map/all_to_all | solution.py:351
  129.3 0.9 reduce_sum.12
  (6 shorter events, 0.0 us)
Async XLA Ops:
  1.8 49.5 %collective-permute-start.2 = (bf16[272,512]{1,0:T(8,128)(2,1)}, bf16[272,512]{1,0:T(8,128)(2,1)S(1)}, u32[]{:S(2)}, u32[]{:S(2)}) collective-permute-start(bf16[272,512]{1,0:T(8,128)(2,1)} %get-tuple-element.15), channel_id=1, source_target_pairs={{384,0},{0,128},{128,256},{256,384},{385,1},{1,129},{129,257},{257... | collective-permute-start | bytes 835592 | tf_op jit(solution)/shard_map/ppermute | solution.py:329
  5.8 45.5 %collective-permute-start.1 = (bf16[272,512]{1,0:T(8,128)(2,1)}, bf16[272,512]{1,0:T(8,128)(2,1)S(1)}, u32[]{:S(2)}, u32[]{:S(2)}) collective-permute-start(bf16[272,512]{1,0:T(8,128)(2,1)} %get-tuple-element.15), channel_id=1, source_target_pairs={{256,0},{384,128},{0,256},{128,384},{257,1},{385,129},{1,257},{129... | collective-permute-start | bytes 835592 | tf_op jit(solution)/shard_map/ppermute | solution.py:329
  10.3 40.9 %collective-permute-start = (bf16[272,512]{1,0:T(8,128)(2,1)}, bf16[272,512]{1,0:T(8,128)(2,1)S(1)}, u32[]{:S(2)}, u32[]{:S(2)}) collective-permute-start(bf16[272,512]{1,0:T(8,128)(2,1)} %get-tuple-element.15), channel_id=1, source_target_pairs={{128,0},{256,128},{384,256},{0,384},{129,1},{257,129},{385,257},{1... | collective-permute-start | bytes 835592 | tf_op jit(solution)/shard_map/ppermute | solution.py:329
  45.9 13.1 %collective-permute-start.3 = (bf16[4,528,128]{2,1,0:T(8,128)(2,1)S(1)}, bf16[4,528,128]{2,1,0:T(8,128)(2,1)S(1)}, u32[]{:S(2)}, u32[]{:S(2)}) collective-permute-start(bf16[4,528,128]{2,1,0:T(8,128)(2,1)S(1)} %bitcast.12), channel_id=1, source_target_pairs={{8,0},{16,8},{24,16},{160,24},{168,160},{176,168},{184,176},{320,1... | collective-permute-start | bytes 1622024 | tf_op jit(solution)/shard_map/ppermute | solution.py:332
  49.0 13.4 %collective-permute-start.4 = (bf16[4,528,128]{2,1,0:T(8,128)(2,1)S(1)}, bf16[4,528,128]{2,1,0:T(8,128)(2,1)S(1)}, u32[]{:S(2)}, u32[]{:S(2)}) collective-permute-start(bf16[4,528,128]{2,1,0:T(8,128)(2,1)S(1)} %bitcast.13), channel_id=1, source_target_pairs={{504,0},{0,8},{8,16},{16,24},{24,160},{160,168},{168,176},{176,184... | collective-permute-start | bytes 1622024 | tf_op jit(solution)/shard_map/ppermute | solution.py:333
  62.5 13.4 %collective-permute-start.5 = (bf16[4,528,128]{2,1,0:T(8,128)(2,1)S(1)}, bf16[4,528,128]{2,1,0:T(8,128)(2,1)S(1)}, u32[]{:S(2)}, u32[]{:S(2)}) collective-permute-start(bf16[4,528,128]{2,1,0:T(8,128)(2,1)S(1)} %broadcast_select_fusion), channel_id=1, source_target_pairs={{8,0},{16,8},{24,16},{160,24},{168,160},{176,168},{184,176},{320,1... | collective-permute-start | bytes 1622024 | tf_op jit(solution)/shard_map/ppermute | solution.py:339
  75.9 4.3 %copy-start = (bf16[512,4096]{1,0:T(8,128)(2,1)S(1)}, bf16[512,4096]{1,0:T(8,128)(2,1)}, u32[]{:S(2)}) copy-start(bf16[512,4096]{1,0:T(8,128)(2,1)} %own_weight.1) | copy-start | bytes 12582916
  80.6 28.6 %collective-permute-start.6 = (bf16[4,512,512]{2,1,0:T(8,128)(2,1)S(1)}, bf16[4,512,512]{2,1,0:T(8,128)(2,1)S(1)}, u32[]{:S(2)}, u32[]{:S(2)}) collective-permute-start(bf16[4,512,512]{2,1,0:T(8,128)(2,1)S(1)} %pack.1), channel_id=1, source_target_pairs={{0,1},{1,0},{2,3},{3,2},{4,5},{5,4},{6,7},{7,6},{8,9},{9,8},{10,11... | collective-permute-start | bytes 6291464 | tf_op jit(solution)/shard_map/ppermute | solution.py:347

commit v7 on v5

--- a/solution.py
+++ b/solution.py
@@ -329,8 +329,8 @@
         lax.ppermute(staged, "y", [((i + n) % NY, i) for i in range(NY)]) for n in (1, 2, 3)
     ]
     own = lax.all_gather(block, ctx, axis=0, axis_index_groups=ring_groups())
+    behind = lax.ppermute(own, ctx, ring_step(-1))
     ahead = lax.ppermute(own, ctx, ring_step(1))
-    behind = lax.ppermute(own, ctx, ring_step(-1))
 
     q_all = jnp.stack([staged, *q_others])
     state = attend((0,), True, False, place, q_all, [own], ())
@@ -338,11 +338,11 @@
     state = (state[0], row_max)
     other_weight = lax.ppermute(pack(core, weight), "core", [(0, 1), (1, 0)])
     far = lax.ppermute(
-        jnp.where(core == 0, ahead, behind),
+        jnp.where(core == 1, behind, ahead),
         (*ctx, "core"),
         [(2 * a + c, 2 * b + c) for c in range(2) for a, b in ring_step(1 - 2 * c)],
     )
-    state = attend((1, -1), False, False, place, q_all, [ahead, behind], state)
+    state = attend((-1, 1), False, False, place, q_all, [behind, ahead], state)
     partial = attend((2,), False, True, place, q_all, [far], state)
     partial = lax.all_to_all(partial, "y", 0, 0, tiled=True)
     both = lax.all_gather(combine(partial), "core", axis=0)

time: 127 us -> 127 us (level)
  waiting for transfers between devices: 6.44 us -> 4.36 us
  starting transfers between devices: 23.4 us -> 25.2 us
    ppermute x1, starting transfers between devices: 1.91 us -> 6.68 us  [local(): ahead = lax.ppermute(own, ctx, ring_step(1))]
    all_gather x1, blocking collectives: 3.82 us -> 6.63 us  [local(): both = lax.all_gather(combine(partial), 'core', axis=0)]
    all_to_all x1, blocking collectives: 16.8 us -> 14.3 us  [local(): partial = lax.all_to_all(partial, 'y', 0, 0, tiled=True)]
    ppermute x1, waiting for transfers between devices: 6.42 us -> 4.34 us  [local(): lax.ppermute(jnp.where(core == 1, behind, ahead), (*ctx, 'core'), [(2 * a...]
    ppermute x1, starting transfers between devices: 5.93 us -> 4.41 us  [local(): other_weight = lax.ppermute(pack(core, weight), 'core', [(0, 1), (1, 0)])]
    ppermute x1, starting transfers between devices: 3.36 us -> 1.91 us  [local(): behind = lax.ppermute(own, ctx, ring_step(-1))]
where the time goes in v7:
time: 127 us
  blocking collectives  75 us (59%)
  starting transfers between devices  25.2 us (20%)
  Pallas kernels  19.9 us (16%)
  waiting for transfers between devices  4.36 us (3%)
  other arithmetic  2.06 us (2%)
    all_gather x1, blocking collectives, local(): own = lax.all_gather(block, ctx, axis=0, axis_index_groups=ring_groups())  36 us
    all_to_all x1, blocking collectives, local(): shares = lax.all_to_all(share, 'x', 0, 0, tiled=True)  18.1 us
    pallas_call x3, Pallas kernels, attend(): pl.pallas_call(functools.partial(attend_kernel, steps, first, last), out_...  15.4 us
    all_to_all x1, blocking collectives, local(): partial = lax.all_to_all(partial, 'y', 0, 0, tiled=True)  14.3 us
    ppermute x3, starting transfers between devices, local(): lax.ppermute(staged, 'y', [((i + n) % NY, i) for i in range(NY)])  10.3 us
    ppermute x1, starting transfers between devices, local(): ahead = lax.ppermute(own, ctx, ring_step(1))  6.68 us
    all_gather x1, blocking collectives, local(): both = lax.all_gather(combine(partial), 'core', axis=0)  6.63 us
    ppermute x1, starting transfers between devices, local(): other_weight = lax.ppermute(pack(core, weight), 'core', [(0, 1), (1, 0)])  4.41 us
  transfers between devices with their start and end apart: 7, of which 1 were waited for; matrix products, arithmetic and copies ran while one was open for 1% of the time, Pallas kernels for 13%

profile of v7, /device:TPU:1, one launch (start us, length us, event | category | flops | bytes accessed | tf_op | source)
XLA Modules:
  0.0 126.8 jit_solution(166876744172619037)
XLA Ops:
  0.0 1.8 %stage.1 = (bf16[272,512]{1,0:T(8,128)(2,1)}, bf16[528,128]{1,0:T(8,128)(2,1)}) custom-call(bf16[256,512]{1,0:T(8,128)(2,1)} %q.1, bf16[256,128]{1,0:T(8,128)(2,1)} %k.1, bf16[256,128]{1,0:T(8,128)(2,1)} %v.1, s32[2,128]{1,0:T(2,128)} %bitcast.19), custom_call_target="tpu_custom_call" | custom-call | tf_op jit(solution)/shard_map/stage/pallas_call | solution.py:309
  1.8 5.5 %collective-permute-start = (bf16[272,512]{1,0:T(8,128)(2,1)}, bf16[272,512]{1,0:T(8,128)(2,1)S(1)}, u32[]{:S(2)}, u32[]{:S(2)}) collective-permute-start(bf16[272,512]{1,0:T(8,128)(2,1)} %get-tuple-element.13), channel_id=1, source_target_pairs={{128,0},{256,128},{384,256},{0,384},{129,1},{257,129},{385,257},{1... | collective-permute-start | bytes 835592 | tf_op jit(solution)/shard_map/ppermute | solution.py:329
  7.2 2.3 %collective-permute-start.1 = (bf16[272,512]{1,0:T(8,128)(2,1)}, bf16[272,512]{1,0:T(8,128)(2,1)S(1)}, u32[]{:S(2)}, u32[]{:S(2)}) collective-permute-start(bf16[272,512]{1,0:T(8,128)(2,1)} %get-tuple-element.13), channel_id=1, source_target_pairs={{256,0},{384,128},{0,256},{128,384},{257,1},{385,129},{1,257},{129... | collective-permute-start | bytes 835592 | tf_op jit(solution)/shard_map/ppermute | solution.py:329
  9.5 2.6 %collective-permute-start.2 = (bf16[272,512]{1,0:T(8,128)(2,1)}, bf16[272,512]{1,0:T(8,128)(2,1)S(1)}, u32[]{:S(2)}, u32[]{:S(2)}) collective-permute-start(bf16[272,512]{1,0:T(8,128)(2,1)} %get-tuple-element.13), channel_id=1, source_target_pairs={{384,0},{0,128},{128,256},{256,384},{385,1},{1,129},{129,257},{257... | collective-permute-start | bytes 835592 | tf_op jit(solution)/shard_map/ppermute | solution.py:329
  12.1 36.0 %all-gather = bf16[2112,128]{1,0:T(8,128)(2,1)S(1)} all-gather(bf16[528,128]{1,0:T(8,128)(2,1)} %get-tuple-element.14), channel_id=2, replica_groups={{0,160,320,480},{8,168,328,488},{16,176,336,496},{24,184,344,504},{32,1..., dimensions={0}, use_global_device_ids=true | all-gather | bytes 675840 | tf_op jit(solution)/shard_map/all_gather | solution.py:331
  48.1 1.9 %collective-permute-start.3 = (bf16[4,528,128]{2,1,0:T(8,128)(2,1)S(1)}, bf16[4,528,128]{2,1,0:T(8,128)(2,1)S(1)}, u32[]{:S(2)}, u32[]{:S(2)}) collective-permute-start(bf16[4,528,128]{2,1,0:T(8,128)(2,1)S(1)} %bitcast.12), channel_id=1, source_target_pairs={{504,0},{0,8},{8,16},{16,24},{24,160},{160,168},{168,176},{176,184... | collective-permute-start | bytes 1622024 | tf_op jit(solution)/shard_map/ppermute | solution.py:332
  50.0 6.7 %collective-permute-start.4 = (bf16[4,528,128]{2,1,0:T(8,128)(2,1)S(1)}, bf16[4,528,128]{2,1,0:T(8,128)(2,1)S(1)}, u32[]{:S(2)}, u32[]{:S(2)}) collective-permute-start(bf16[4,528,128]{2,1,0:T(8,128)(2,1)S(1)} %bitcast.13), channel_id=1, source_target_pairs={{8,0},{16,8},{24,16},{160,24},{168,160},{176,168},{184,176},{320,1... | collective-permute-start | bytes 1622024 | tf_op jit(solution)/shard_map/ppermute | solution.py:333
  56.7 0.0 collective-permute-done
  56.8 1.1 pad_maximum_fusion.q_ref
  57.9 0.0 copy-start
  57.9 3.9 %attend.3 = (f32[4,4,144,256]{3,2,1,0:T(8,128)S(1)}, f32[4,4,1,256]{3,2,1,0:T(1,128)S(1)}) custom-call(s32[1]{0:T(128)} %bitcast.1.y_ref, s32[1]{0:T(128)} %bitcast.2.z_ref, bf16[4,272,512]{2,1,0:T(8,128)(2,1)S(1)} %pad_maximum_fusion.q_ref, bf16[4,528,128]{2,1,0:T(8,128)(2,1)S(1)} %bitcast.14), custom_call_target="tpu_custom_call" | custom-call | flops 2684354560 | bytes 6291456 | tf_op jit(solution)/shard_map/attend/pallas_call | solution.py:196
  61.8 0.4 pack.1
  62.3 4.4 %collective-permute-start.6 = (bf16[4,512,512]{2,1,0:T(8,128)(2,1)S(1)}, bf16[4,512,512]{2,1,0:T(8,128)(2,1)S(1)}, u32[]{:S(2)}, u32[]{:S(2)}) collective-permute-start(bf16[4,512,512]{2,1,0:T(8,128)(2,1)S(1)} %pack.1), channel_id=1, source_target_pairs={{0,1},{1,0},{2,3},{3,2},{4,5},{5,4},{6,7},{7,6},{8,9},{9,8},{10,11... | collective-permute-start | bytes 6291464 | tf_op jit(solution)/shard_map/ppermute | solution.py:339
  66.7 0.1 broadcast_select_fusion
  66.8 1.9 %collective-permute-start.5 = (bf16[4,528,128]{2,1,0:T(8,128)(2,1)S(1)}, bf16[4,528,128]{2,1,0:T(8,128)(2,1)S(1)}, u32[]{:S(2)}, u32[]{:S(2)}) collective-permute-start(bf16[4,528,128]{2,1,0:T(8,128)(2,1)S(1)} %broadcast_select_fusion), channel_id=1, source_target_pairs={{8,0},{16,8},{24,16},{160,24},{168,160},{176,168},{184,176},{320,1... | collective-permute-start | bytes 1622024 | tf_op jit(solution)/shard_map/ppermute | solution.py:340
  68.7 7.2 %attend.4 = (f32[4,4,144,256]{3,2,1,0:T(8,128)S(1)}, f32[4,4,1,256]{3,2,1,0:T(1,128)S(1)}) custom-call(s32[1]{0:T(128)} %bitcast.1.y_ref, s32[1]{0:T(128)} %bitcast.2.z_ref, bf16[4,272,512]{2,1,0:T(8,128)(2,1)S(1)} %pad_maximum_fusion.q_ref, bf16[4,528,128]{2,1,0:T(8,128)(2,1)S(1)} %collective-permute-done.3.refs_0_, ...), custom_call_target="tpu_custom_call", output_to_operand_aliasing={{0}: (5, {}), {1}: (6, {})} | custom-call | flops 5368709120 | bytes 6291456 | tf_op jit(solution)/shard_map/attend/pallas_call | solution.py:196
  75.9 4.3 %collective-permute-done.5.refs_0_ = bf16[4,528,128]{2,1,0:T(8,128)(2,1)S(1)} collective-permute-done((bf16[4,528,128]{2,1,0:T(8,128)(2,1)S(1)}, bf16[4,528,128]{2,1,0:T(8,128)(2,1)S(1)}, u32[]{:S(2)}, u32[]{:S(2)}) %collective-permute-start.5) | collective-permute-done | bytes 540704 | tf_op jit(solution)/shard_map/ppermute | solution.py:340
  80.3 4.3 %attend.5 = bf16[4,528,256]{2,1,0:T(8,128)(2,1)S(1)} custom-call(s32[1]{0:T(128)} %bitcast.1.y_ref, s32[1]{0:T(128)} %bitcast.2.z_ref, bf16[4,272,512]{2,1,0:T(8,128)(2,1)S(1)} %pad_maximum_fusion.q_ref, bf16[4,528,128]{2,1,0:T(8,128)(2,1)S(1)} %collective-permute-done.5.refs_0_, f32[4,4,144,256]{3,2,1,0:T(8,128)S(1)} %get-tuple-element.18.refs_1_, ...), custom_call_target="tpu_custom_call" | custom-call | flops 2684354560 | bytes 6291456 | tf_op jit(solution)/shard_map/attend/pallas_call | solution.py:196
  84.5 14.3 %all_to_all.10.parts = bf16[4,528,256]{2,1,0:T(8,128)(2,1)S(1)} all-to-all(bf16[4,528,256]{2,1,0:T(8,128)(2,1)S(1)} %attend.5), channel_id=1, replica_groups=mesh['y'=4,'z'=16,'x'=4,'core'=2] {'y'}, dimensions={0} | all-to-all | bytes 2162688 | tf_op jit(solution)/shard_map/all_to_all | solution.py:347
  98.9 0.3 combine.1
  99.2 6.6 %all-gather.1 = bf16[512,512]{1,0:T(8,128)(2,1)S(1)} all-gather(bf16[256,512]{1,0:T(8,128)(2,1)S(1)} %combine.1), channel_id=3, replica_groups=mesh['y'=4,'z'=16,'x'=4,'core'=2] {'core'}, dimensions={0}, use_global_device_ids=true | all-gather | bytes 786432 | tf_op jit(solution)/shard_map/all_gather | solution.py:348
  105.8 2.0 %project.1 = bf16[4,256,512]{2,1,0:T(8,128)(2,1)S(1)} custom-call(s32[1]{0:T(128)} %bitcast.core, bf16[2,256,512]{2,1,0:T(8,128)(2,1)S(1)} %bitcast.11, bf16[512,4096]{1,0:T(8,128)(2,1)S(1)} %copy-done, bf16[4,512,512]{2,1,0:T(8,128)(2,1)S(1)} %collective-permute-done.6.other_weight), custom_call_target="tpu_custom_call" | custom-call | tf_op jit(solution)/shard_map/project/pallas_call | solution.py:275
  107.8 18.1 %all_to_all.11 = bf16[4,256,512]{2,1,0:T(8,128)(2,1)S(1)} all-to-all(bf16[4,256,512]{2,1,0:T(8,128)(2,1)S(1)} %project.1), channel_id=1, replica_groups=mesh['y'=4,'z'=16,'x'=4,'core'=2] {'x'}, dimensions={0} | all-to-all | bytes 2097152 | tf_op jit(solution)/shard_map/all_to_all | solution.py:350
  125.8 0.9 reduce_sum.12
  (6 shorter events, 0.0 us)
Async XLA Ops:
  1.8 55.0 %collective-permute-start = (bf16[272,512]{1,0:T(8,128)(2,1)}, bf16[272,512]{1,0:T(8,128)(2,1)S(1)}, u32[]{:S(2)}, u32[]{:S(2)}) collective-permute-start(bf16[272,512]{1,0:T(8,128)(2,1)} %get-tuple-element.13), channel_id=1, source_target_pairs={{128,0},{256,128},{384,256},{0,384},{129,1},{257,129},{385,257},{1... | collective-permute-start | bytes 835592 | tf_op jit(solution)/shard_map/ppermute | solution.py:329
  7.2 49.5 %collective-permute-start.1 = (bf16[272,512]{1,0:T(8,128)(2,1)}, bf16[272,512]{1,0:T(8,128)(2,1)S(1)}, u32[]{:S(2)}, u32[]{:S(2)}) collective-permute-start(bf16[272,512]{1,0:T(8,128)(2,1)} %get-tuple-element.13), channel_id=1, source_target_pairs={{256,0},{384,128},{0,256},{128,384},{257,1},{385,129},{1,257},{129... | collective-permute-start | bytes 835592 | tf_op jit(solution)/shard_map/ppermute | solution.py:329
  9.5 47.3 %collective-permute-start.2 = (bf16[272,512]{1,0:T(8,128)(2,1)}, bf16[272,512]{1,0:T(8,128)(2,1)S(1)}, u32[]{:S(2)}, u32[]{:S(2)}) collective-permute-start(bf16[272,512]{1,0:T(8,128)(2,1)} %get-tuple-element.13), channel_id=1, source_target_pairs={{384,0},{0,128},{128,256},{256,384},{385,1},{1,129},{129,257},{257... | collective-permute-start | bytes 835592 | tf_op jit(solution)/shard_map/ppermute | solution.py:329
  48.1 18.6 %collective-permute-start.3 = (bf16[4,528,128]{2,1,0:T(8,128)(2,1)S(1)}, bf16[4,528,128]{2,1,0:T(8,128)(2,1)S(1)}, u32[]{:S(2)}, u32[]{:S(2)}) collective-permute-start(bf16[4,528,128]{2,1,0:T(8,128)(2,1)S(1)} %bitcast.12), channel_id=1, source_target_pairs={{504,0},{0,8},{8,16},{16,24},{24,160},{160,168},{168,176},{176,184... | collective-permute-start | bytes 1622024 | tf_op jit(solution)/shard_map/ppermute | solution.py:332
  50.0 16.6 %collective-permute-start.4 = (bf16[4,528,128]{2,1,0:T(8,128)(2,1)S(1)}, bf16[4,528,128]{2,1,0:T(8,128)(2,1)S(1)}, u32[]{:S(2)}, u32[]{:S(2)}) collective-permute-start(bf16[4,528,128]{2,1,0:T(8,128)(2,1)S(1)} %bitcast.13), channel_id=1, source_target_pairs={{8,0},{16,8},{24,16},{160,24},{168,160},{176,168},{184,176},{320,1... | collective-permute-start | bytes 1622024 | tf_op jit(solution)/shard_map/ppermute | solution.py:333
  57.9 4.0 %copy-start = (bf16[512,4096]{1,0:T(8,128)(2,1)S(1)}, bf16[512,4096]{1,0:T(8,128)(2,1)}, u32[]{:S(2)}) copy-start(bf16[512,4096]{1,0:T(8,128)(2,1)} %own_weight.1) | copy-start | bytes 12582916
  62.3 43.5 %collective-permute-start.6 = (bf16[4,512,512]{2,1,0:T(8,128)(2,1)S(1)}, bf16[4,512,512]{2,1,0:T(8,128)(2,1)S(1)}, u32[]{:S(2)}, u32[]{:S(2)}) collective-permute-start(bf16[4,512,512]{2,1,0:T(8,128)(2,1)S(1)} %pack.1), channel_id=1, source_target_pairs={{0,1},{1,0},{2,3},{3,2},{4,5},{5,4},{6,7},{7,6},{8,9},{9,8},{10,11... | collective-permute-start | bytes 6291464 | tf_op jit(solution)/shard_map/ppermute | solution.py:339
  66.8 13.5 %collective-permute-start.5 = (bf16[4,528,128]{2,1,0:T(8,128)(2,1)S(1)}, bf16[4,528,128]{2,1,0:T(8,128)(2,1)S(1)}, u32[]{:S(2)}, u32[]{:S(2)}) collective-permute-start(bf16[4,528,128]{2,1,0:T(8,128)(2,1)S(1)} %broadcast_select_fusion), channel_id=1, source_target_pairs={{8,0},{16,8},{24,16},{160,24},{168,160},{176,168},{184,176},{320,1... | collective-permute-start | bytes 1622024 | tf_op jit(solution)/shard_map/ppermute | solution.py:340

commit v8 on v5

--- a/solution.py
+++ b/solution.py
@@ -326,13 +326,13 @@
 
     staged, block = stage(queries, keys, values, block_ids.reshape(2, 128))
     q_others = [
-        lax.ppermute(staged, "y", [((i + n) % NY, i) for i in range(NY)]) for n in (1, 2, 3)
+        lax.ppermute(staged, "y", [((i + n) % NY, i) for i in range(NY)]) for n in (1, 3, 2)
     ]
     own = lax.all_gather(block, ctx, axis=0, axis_index_groups=ring_groups())
     ahead = lax.ppermute(own, ctx, ring_step(1))
     behind = lax.ppermute(own, ctx, ring_step(-1))
 
-    q_all = jnp.stack([staged, *q_others])
+    q_all = jnp.stack([staged, q_others[0], q_others[2], q_others[1]])
     state = attend((0,), True, False, place, q_all, [own], ())
     weight, row_max = lax.optimization_barrier((out_weight, state[1]))
     state = (state[0], row_max)

time: 127 us -> 127 us (level)
  no operation moved by 1% of the time
where the time goes in v8:
time: 127 us
  blocking collectives  74.7 us (59%)
  starting transfers between devices  23.4 us (18%)
  Pallas kernels  19.9 us (16%)
  waiting for transfers between devices  6.44 us (5%)
  other arithmetic  2.06 us (2%)
    all_gather x1, blocking collectives, local(): own = lax.all_gather(block, ctx, axis=0, axis_index_groups=ring_groups())  36 us
    all_to_all x1, blocking collectives, local(): shares = lax.all_to_all(share, 'x', 0, 0, tiled=True)  18.1 us
    all_to_all x1, blocking collectives, local(): partial = lax.all_to_all(partial, 'y', 0, 0, tiled=True)  16.8 us
    pallas_call x3, Pallas kernels, attend(): pl.pallas_call(functools.partial(attend_kernel, steps, first, last), out_...  15.4 us
    ppermute x3, starting transfers between devices, local(): lax.ppermute(staged, 'y', [((i + n) % NY, i) for i in range(NY)])  10.3 us
    ppermute x1, waiting for transfers between devices, local(): lax.ppermute(jnp.where(core == 0, ahead, behind), (*ctx, 'core'), [(2 * a...  6.42 us
    ppermute x1, starting transfers between devices, local(): other_weight = lax.ppermute(pack(core, weight), 'core', [(0, 1), (1, 0)])  5.93 us
    all_gather x1, blocking collectives, local(): both = lax.all_gather(combine(partial), 'core', axis=0)  3.82 us
  transfers between devices with their start and end apart: 7, of which 1 were waited for; matrix products, arithmetic and copies ran while one was open for 1% of the time, Pallas kernels for 13%

profile of v8, /device:TPU:1, one launch (start us, length us, event | category | flops | bytes accessed | tf_op | source)
XLA Modules:
  0.0 126.7 jit_solution(846973493872755519)
XLA Ops:
  0.0 1.8 %stage.1 = (bf16[272,512]{1,0:T(8,128)(2,1)}, bf16[528,128]{1,0:T(8,128)(2,1)}) custom-call(bf16[256,512]{1,0:T(8,128)(2,1)} %q.1, bf16[256,128]{1,0:T(8,128)(2,1)} %k.1, bf16[256,128]{1,0:T(8,128)(2,1)} %v.1, s32[2,128]{1,0:T(2,128)} %bitcast.19), custom_call_target="tpu_custom_call" | custom-call | tf_op jit(solution)/shard_map/stage/pallas_call | solution.py:309
  1.8 5.5 %collective-permute-start = (bf16[272,512]{1,0:T(8,128)(2,1)}, bf16[272,512]{1,0:T(8,128)(2,1)S(1)}, u32[]{:S(2)}, u32[]{:S(2)}) collective-permute-start(bf16[272,512]{1,0:T(8,128)(2,1)} %get-tuple-element.13), channel_id=1, source_target_pairs={{128,0},{256,128},{384,256},{0,384},{129,1},{257,129},{385,257},{1... | collective-permute-start | bytes 835592 | tf_op jit(solution)/shard_map/ppermute | solution.py:329
  7.2 2.3 %collective-permute-start.1 = (bf16[272,512]{1,0:T(8,128)(2,1)}, bf16[272,512]{1,0:T(8,128)(2,1)S(1)}, u32[]{:S(2)}, u32[]{:S(2)}) collective-permute-start(bf16[272,512]{1,0:T(8,128)(2,1)} %get-tuple-element.13), channel_id=1, source_target_pairs={{256,0},{384,128},{0,256},{128,384},{257,1},{385,129},{1,257},{129... | collective-permute-start | bytes 835592 | tf_op jit(solution)/shard_map/ppermute | solution.py:329
  9.5 2.6 %collective-permute-start.2 = (bf16[272,512]{1,0:T(8,128)(2,1)}, bf16[272,512]{1,0:T(8,128)(2,1)S(1)}, u32[]{:S(2)}, u32[]{:S(2)}) collective-permute-start(bf16[272,512]{1,0:T(8,128)(2,1)} %get-tuple-element.13), channel_id=1, source_target_pairs={{384,0},{0,128},{128,256},{256,384},{385,1},{1,129},{129,257},{257... | collective-permute-start | bytes 835592 | tf_op jit(solution)/shard_map/ppermute | solution.py:329
  12.1 36.0 %all-gather = bf16[2112,128]{1,0:T(8,128)(2,1)S(1)} all-gather(bf16[528,128]{1,0:T(8,128)(2,1)} %get-tuple-element.14), channel_id=2, replica_groups={{0,160,320,480},{8,168,328,488},{16,176,336,496},{24,184,344,504},{32,1..., dimensions={0}, use_global_device_ids=true | all-gather | bytes 675840 | tf_op jit(solution)/shard_map/all_gather | solution.py:331
  48.1 1.9 %collective-permute-start.3 = (bf16[4,528,128]{2,1,0:T(8,128)(2,1)S(1)}, bf16[4,528,128]{2,1,0:T(8,128)(2,1)S(1)}, u32[]{:S(2)}, u32[]{:S(2)}) collective-permute-start(bf16[4,528,128]{2,1,0:T(8,128)(2,1)S(1)} %bitcast.12), channel_id=1, source_target_pairs={{8,0},{16,8},{24,16},{160,24},{168,160},{176,168},{184,176},{320,1... | collective-permute-start | bytes 1622024 | tf_op jit(solution)/shard_map/ppermute | solution.py:332
  50.0 3.4 %collective-permute-start.4 = (bf16[4,528,128]{2,1,0:T(8,128)(2,1)S(1)}, bf16[4,528,128]{2,1,0:T(8,128)(2,1)S(1)}, u32[]{:S(2)}, u32[]{:S(2)}) collective-permute-start(bf16[4,528,128]{2,1,0:T(8,128)(2,1)S(1)} %bitcast.13), channel_id=1, source_target_pairs={{504,0},{0,8},{8,16},{16,24},{24,160},{160,168},{168,176},{176,184... | collective-permute-start | bytes 1622024 | tf_op jit(solution)/shard_map/ppermute | solution.py:333
  53.4 0.0 collective-permute-done
  53.4 1.1 pad_maximum_fusion.q_ref
  54.5 0.0 copy-start
  54.6 3.9 %attend.3 = (f32[4,4,144,256]{3,2,1,0:T(8,128)S(1)}, f32[4,4,1,256]{3,2,1,0:T(1,128)S(1)}) custom-call(s32[1]{0:T(128)} %bitcast.1.y_ref, s32[1]{0:T(128)} %bitcast.2.z_ref, bf16[4,272,512]{2,1,0:T(8,128)(2,1)S(1)} %pad_maximum_fusion.q_ref, bf16[4,528,128]{2,1,0:T(8,128)(2,1)S(1)} %bitcast.14), custom_call_target="tpu_custom_call" | custom-call | flops 2684354560 | bytes 6291456 | tf_op jit(solution)/shard_map/attend/pallas_call | solution.py:196
  58.5 0.4 pack.1
  58.9 5.9 %collective-permute-start.6 = (bf16[4,512,512]{2,1,0:T(8,128)(2,1)S(1)}, bf16[4,512,512]{2,1,0:T(8,128)(2,1)S(1)}, u32[]{:S(2)}, u32[]{:S(2)}) collective-permute-start(bf16[4,512,512]{2,1,0:T(8,128)(2,1)S(1)} %pack.1), channel_id=1, source_target_pairs={{0,1},{1,0},{2,3},{3,2},{4,5},{5,4},{6,7},{7,6},{8,9},{9,8},{10,11... | collective-permute-start | bytes 6291464 | tf_op jit(solution)/shard_map/ppermute | solution.py:339
  64.9 0.1 broadcast_select_fusion
  65.0 1.9 %collective-permute-start.5 = (bf16[4,528,128]{2,1,0:T(8,128)(2,1)S(1)}, bf16[4,528,128]{2,1,0:T(8,128)(2,1)S(1)}, u32[]{:S(2)}, u32[]{:S(2)}) collective-permute-start(bf16[4,528,128]{2,1,0:T(8,128)(2,1)S(1)} %broadcast_select_fusion), channel_id=1, source_target_pairs={{8,0},{16,8},{24,16},{160,24},{168,160},{176,168},{184,176},{320,1... | collective-permute-start | bytes 1622024 | tf_op jit(solution)/shard_map/ppermute | solution.py:340
  66.9 7.2 %attend.4 = (f32[4,4,144,256]{3,2,1,0:T(8,128)S(1)}, f32[4,4,1,256]{3,2,1,0:T(1,128)S(1)}) custom-call(s32[1]{0:T(128)} %bitcast.1.y_ref, s32[1]{0:T(128)} %bitcast.2.z_ref, bf16[4,272,512]{2,1,0:T(8,128)(2,1)S(1)} %pad_maximum_fusion.q_ref, bf16[4,528,128]{2,1,0:T(8,128)(2,1)S(1)} %collective-permute-done.3.refs_0_, ...), custom_call_target="tpu_custom_call", output_to_operand_aliasing={{0}: (5, {}), {1}: (6, {})} | custom-call | flops 5368709120 | bytes 6291456 | tf_op jit(solution)/shard_map/attend/pallas_call | solution.py:196
  74.2 6.4 %collective-permute-done.5.refs_0_ = bf16[4,528,128]{2,1,0:T(8,128)(2,1)S(1)} collective-permute-done((bf16[4,528,128]{2,1,0:T(8,128)(2,1)S(1)}, bf16[4,528,128]{2,1,0:T(8,128)(2,1)S(1)}, u32[]{:S(2)}, u32[]{:S(2)}) %collective-permute-start.5) | collective-permute-done | bytes 540704 | tf_op jit(solution)/shard_map/ppermute | solution.py:340
  80.6 4.3 %attend.5 = bf16[4,528,256]{2,1,0:T(8,128)(2,1)S(1)} custom-call(s32[1]{0:T(128)} %bitcast.1.y_ref, s32[1]{0:T(128)} %bitcast.2.z_ref, bf16[4,272,512]{2,1,0:T(8,128)(2,1)S(1)} %pad_maximum_fusion.q_ref, bf16[4,528,128]{2,1,0:T(8,128)(2,1)S(1)} %collective-permute-done.5.refs_0_, f32[4,4,144,256]{3,2,1,0:T(8,128)S(1)} %get-tuple-element.18.refs_1_, ...), custom_call_target="tpu_custom_call" | custom-call | flops 2684354560 | bytes 6291456 | tf_op jit(solution)/shard_map/attend/pallas_call | solution.py:196
  84.8 16.8 %all_to_all.10.parts = bf16[4,528,256]{2,1,0:T(8,128)(2,1)S(1)} all-to-all(bf16[4,528,256]{2,1,0:T(8,128)(2,1)S(1)} %attend.5), channel_id=1, replica_groups=mesh['y'=4,'z'=16,'x'=4,'core'=2] {'y'}, dimensions={0} | all-to-all | bytes 2162688 | tf_op jit(solution)/shard_map/all_to_all | solution.py:347
  101.6 0.3 combine.1
  101.9 3.8 %all-gather.1 = bf16[512,512]{1,0:T(8,128)(2,1)S(1)} all-gather(bf16[256,512]{1,0:T(8,128)(2,1)S(1)} %combine.1), channel_id=3, replica_groups=mesh['y'=4,'z'=16,'x'=4,'core'=2] {'core'}, dimensions={0}, use_global_device_ids=true | all-gather | bytes 786432 | tf_op jit(solution)/shard_map/all_gather | solution.py:348
  105.7 2.0 %project.1 = bf16[4,256,512]{2,1,0:T(8,128)(2,1)S(1)} custom-call(s32[1]{0:T(128)} %bitcast.core, bf16[2,256,512]{2,1,0:T(8,128)(2,1)S(1)} %bitcast.11, bf16[512,4096]{1,0:T(8,128)(2,1)S(1)} %copy-done, bf16[4,512,512]{2,1,0:T(8,128)(2,1)S(1)} %collective-permute-done.6.other_weight), custom_call_target="tpu_custom_call" | custom-call | tf_op jit(solution)/shard_map/project/pallas_call | solution.py:275
  107.7 18.1 %all_to_all.11 = bf16[4,256,512]{2,1,0:T(8,128)(2,1)S(1)} all-to-all(bf16[4,256,512]{2,1,0:T(8,128)(2,1)S(1)} %project.1), channel_id=1, replica_groups=mesh['y'=4,'z'=16,'x'=4,'core'=2] {'x'}, dimensions={0} | all-to-all | bytes 2097152 | tf_op jit(solution)/shard_map/all_to_all | solution.py:350
  125.8 0.9 reduce_sum.12
  (6 shorter events, 0.0 us)
Async XLA Ops:
  1.8 51.7 %collective-permute-start = (bf16[272,512]{1,0:T(8,128)(2,1)}, bf16[272,512]{1,0:T(8,128)(2,1)S(1)}, u32[]{:S(2)}, u32[]{:S(2)}) collective-permute-start(bf16[272,512]{1,0:T(8,128)(2,1)} %get-tuple-element.13), channel_id=1, source_target_pairs={{128,0},{256,128},{384,256},{0,384},{129,1},{257,129},{385,257},{1... | collective-permute-start | bytes 835592 | tf_op jit(solution)/shard_map/ppermute | solution.py:329
  7.2 46.2 %collective-permute-start.1 = (bf16[272,512]{1,0:T(8,128)(2,1)}, bf16[272,512]{1,0:T(8,128)(2,1)S(1)}, u32[]{:S(2)}, u32[]{:S(2)}) collective-permute-start(bf16[272,512]{1,0:T(8,128)(2,1)} %get-tuple-element.13), channel_id=1, source_target_pairs={{256,0},{384,128},{0,256},{128,384},{257,1},{385,129},{1,257},{129... | collective-permute-start | bytes 835592 | tf_op jit(solution)/shard_map/ppermute | solution.py:329
  9.5 43.9 %collective-permute-start.2 = (bf16[272,512]{1,0:T(8,128)(2,1)}, bf16[272,512]{1,0:T(8,128)(2,1)S(1)}, u32[]{:S(2)}, u32[]{:S(2)}) collective-permute-start(bf16[272,512]{1,0:T(8,128)(2,1)} %get-tuple-element.13), channel_id=1, source_target_pairs={{384,0},{0,128},{128,256},{256,384},{385,1},{1,129},{129,257},{257... | collective-permute-start | bytes 835592 | tf_op jit(solution)/shard_map/ppermute | solution.py:329
  48.1 16.8 %collective-permute-start.3 = (bf16[4,528,128]{2,1,0:T(8,128)(2,1)S(1)}, bf16[4,528,128]{2,1,0:T(8,128)(2,1)S(1)}, u32[]{:S(2)}, u32[]{:S(2)}) collective-permute-start(bf16[4,528,128]{2,1,0:T(8,128)(2,1)S(1)} %bitcast.12), channel_id=1, source_target_pairs={{8,0},{16,8},{24,16},{160,24},{168,160},{176,168},{184,176},{320,1... | collective-permute-start | bytes 1622024 | tf_op jit(solution)/shard_map/ppermute | solution.py:332
  50.0 14.9 %collective-permute-start.4 = (bf16[4,528,128]{2,1,0:T(8,128)(2,1)S(1)}, bf16[4,528,128]{2,1,0:T(8,128)(2,1)S(1)}, u32[]{:S(2)}, u32[]{:S(2)}) collective-permute-start(bf16[4,528,128]{2,1,0:T(8,128)(2,1)S(1)} %bitcast.13), channel_id=1, source_target_pairs={{504,0},{0,8},{8,16},{16,24},{24,160},{160,168},{168,176},{176,184... | collective-permute-start | bytes 1622024 | tf_op jit(solution)/shard_map/ppermute | solution.py:333
  54.5 4.0 %copy-start = (bf16[512,4096]{1,0:T(8,128)(2,1)S(1)}, bf16[512,4096]{1,0:T(8,128)(2,1)}, u32[]{:S(2)}) copy-start(bf16[512,4096]{1,0:T(8,128)(2,1)} %own_weight.1) | copy-start | bytes 12582916
  58.9 46.8 %collective-permute-start.6 = (bf16[4,512,512]{2,1,0:T(8,128)(2,1)S(1)}, bf16[4,512,512]{2,1,0:T(8,128)(2,1)S(1)}, u32[]{:S(2)}, u32[]{:S(2)}) collective-permute-start(bf16[4,512,512]{2,1,0:T(8,128)(2,1)S(1)} %pack.1), channel_id=1, source_target_pairs={{0,1},{1,0},{2,3},{3,2},{4,5},{5,4},{6,7},{7,6},{8,9},{9,8},{10,11... | collective-permute-start | bytes 6291464 | tf_op jit(solution)/shard_map/ppermute | solution.py:339
  65.0 15.6 %collective-permute-start.5 = (bf16[4,528,128]{2,1,0:T(8,128)(2,1)S(1)}, bf16[4,528,128]{2,1,0:T(8,128)(2,1)S(1)}, u32[]{:S(2)}, u32[]{:S(2)}) collective-permute-start(bf16[4,528,128]{2,1,0:T(8,128)(2,1)S(1)} %broadcast_select_fusion), channel_id=1, source_target_pairs={{8,0},{16,8},{24,16},{160,24},{168,160},{176,168},{184,176},{320,1... | collective-permute-start | bytes 1622024 | tf_op jit(solution)/shard_map/ppermute | solution.py:340
